TPU v7x, 128 devices: a whole 4x4x4 slice. The times are simulated.
128 devices in a mesh: stream: 8 (over y_lo, z), span: 4 (over y_hi, core), depth: 4 (over x).
Axes of the slice: x: 4, y: 4 (y_hi: 2, y_lo: 2; y = y_hi * 2 + y_lo), z: 4, core: 2. Of those that a mesh axis runs over, the one named last changes fastest.
Arguments:
- fluid_velocity: float32 [256, 128, 512], P('stream', 'depth', 'span'), may hold values from 0.2 to 1.5
- fluid_temp: float32 [256, 128, 512], P('stream', 'depth', 'span'), may hold values from -6 to 6
- solid_temp: float32 [256, 64, 512], P('stream', None, 'span'), may hold values from -6 to 6
- channel_mask: int32 [256, 512], P('stream', 'span'), may hold values 0 or 1
- owner_shift: int32 [512], P('span'), may hold values from 0 to 255
Outputs:
- new_velocity: float32 [256, 128, 512], P('stream', 'depth', 'span')
- new_fluid_temp: float32 [256, 128, 512], P('stream', 'depth', 'span')
- new_solid_temp: float32 [256, 64, 512], P('stream', None, 'span')
- wall_temp: float32 [256, 512], P('stream', ('span', 'depth'))
Inputs may be any that keep to these rules, and one draw needn't show every extreme that they name: Wall faces lie at wall-normal cell 0 of the fluid; face (s, w) is owned by copper row (s + owner_shift[w]) mod 256 of column w.
All inputs are finite; a program needn't handle non-finite values. No bound on the sum of `channel_mask` on one device may be relied on, other than what follows from the above.
Results may differ from a plain program's by a relative error of at most 0.000068.
Values sent between devices are 32-bit elements; how exact they have to be, the bound alone decides.
A program may use at most 64 MiB of HBM per device.

v0:
```python
import functools
import math

import jax
import jax.numpy as jnp
from jax import lax
from jax.experimental import pallas as pl
from jax.experimental.pallas import tpu as pltpu
from jax.sharding import PartitionSpec as P

SWEEPS = 6
VISCOSITY = 0.1
DIFFUSIVITY = 0.15
ADVECTION = 0.2
TRANSFER = 0.5

LANES = 128
ROWS = 32
CELLS = 32
LAYERS = 64
EXT = ROWS + 2 * SWEEPS
HALF = ROWS // 2
STRIP = HALF + 2 * SWEEPS
PACK = 21
SOURCE_ROWS = 48

V_UP, V_DOWN, T_UP, T_DOWN = 0, 1, 2, 3
N_UP, N_DOWN = 4, 5
W_UP, W_DOWN = 6, 7
T0_UP, T0_DOWN = 8, 9
C_UP, C_DOWN = 10, 11
E_UP, E_DOWN = 12, 13
S_UP, S_DOWN = 14, 15
GATHER = 16


def weight(sweep):
    return 1.0 / (1.0 + 6.0 / 7.0 * math.cos(math.pi * (2 * sweep + 1) / (2 * SWEEPS)))


def lane_of(shape):
    return lax.broadcasted_iota(jnp.int32, shape, len(shape) - 1)


def sub_of(shape):
    return lax.broadcasted_iota(jnp.int32, shape, len(shape) - 2)


def roll(x, shift, axis=None):
    axis = x.ndim - 1 if axis is None else axis
    if isinstance(shift, int):
        shift = shift % x.shape[axis]
        if shift == 0:
            return x
    return pltpu.roll(x, shift, axis)


def route(plane, amount, wanted):
    total = plane.shape[0]
    amount = amount & (total - 1)
    step = total // 2
    plane = jnp.concatenate((plane, plane[:wanted]), axis=0)
    while step >= 8:
        keep = wanted + step
        bits = jnp.broadcast_to(amount, (keep, LANES)) & step
        plane = jnp.where(bits != 0, plane[step : step + keep], plane[:keep])
        step //= 2
    keep = wanted + 8
    while step >= 1:
        bits = jnp.broadcast_to(amount, (keep, LANES)) & step
        plane = jnp.where(bits != 0, roll(plane, keep - step, 0), plane)
        step //= 2
    return plane[:wanted]


def regions(lane, parts):
    out = parts[7]
    for n in range(6, -1, -1):
        out = jnp.where(lane < 16 * (n + 1), parts[n], out)
    return out


def rows_loop(first, last, unroll, body, carry):
    count = (last - first) // unroll

    def several(n, carry):
        for u in range(unroll):
            carry = body(first + n * unroll + u, carry)
        return carry

    carry = lax.fori_loop(0, count, several, carry)
    for row in range(first + count * unroll, last):
        carry = body(row, carry)
    return carry


def copper_sweep(out, src, rhs, first, last, sweep):
    omega = weight(sweep)
    keep, gain = 1.0 - omega, omega / 7.0
    sub = sub_of((1, 8, LANES))

    def body(row, carry):
        prev, cur = carry
        nxt = src[row + 1]
        side = roll(cur, 1) + roll(cur, LANES - 1)
        up = jnp.concatenate(
            (cur[1:], jnp.where(sub == 7, 0.0, roll(cur[:1], 7, 1))), axis=0
        )
        down = jnp.concatenate(
            (jnp.where(sub == 0, cur[:1], roll(cur[7:], 1, 1)), cur[:7]), axis=0
        )
        near = (prev + nxt) + (up + down) + side
        out[row] = keep * cur + gain * (rhs[row] + near)
        return cur, nxt

    rows_loop(first, last, 2, body, (src[first - 1], src[first]))


def source_sweep(state, source, first, last, sweep):
    omega = weight(sweep)
    keep, gain = 1.0 - omega, omega / 7.0
    sub = sub_of((8, LANES))

    def fed(row):
        return jnp.where(sub == 0, jnp.broadcast_to(source[pl.ds(row, 1), :], (8, LANES)), 0.0)

    if sweep == 0:

        def begin(row, carry):
            state[row] = gain * fed(row)
            return carry

        rows_loop(first, last, 6, begin, 0)
        return

    def body(row, carry):
        prev, cur = carry
        nxt = state[row + 1]
        side = roll(cur, 1) + roll(cur, LANES - 1)
        up = jnp.where(sub == 7, 0.0, roll(cur, 7, 0))
        down = jnp.where(sub == 0, cur, roll(cur, 1, 0))
        near = (prev + nxt) + (up + down) + side
        state[row] = keep * cur + gain * (fed(row) + near)
        return cur, nxt

    rows_loop(first, last, 8, body, (state[first - 1], state[first]))


def with_edges(lane, main, strip, half):
    low, high = (roll(strip, 0), roll(strip, 96)) if half == 0 else (roll(strip, 64), roll(strip, 32))
    return jnp.where(lane < SWEEPS, low, jnp.where(lane >= LANES - SWEEPS, high, main))


def kernel(
    v_in,
    t_in,
    c_in,
    mask_ref,
    shift_ref,
    v_out,
    t_out,
    c_out,
    wall_ref,
    vb,
    tb,
    xn,
    rm,
    xm,
    rs,
    xs,
    oc,
    ov,
    ot,
    n_send,
    n_recv,
    w_send,
    w_recv,
    t0_recv,
    e_send,
    e_recv,
    surface,
    flux,
    face,
    source,
    strip_source,
    gm,
    gs,
    wall_send,
    wall_all,
    below,
    send_sem,
    recv_sem,
    local_sem,
):
    streams, spans, depths = (lax.axis_size(a) for a in ("stream", "span", "depth"))
    i, j, k = (lax.axis_index(a) for a in ("stream", "span", "depth"))
    up_i, down_i = lax.rem(i + 1, streams), lax.rem(i + streams - 1, streams)
    up_j, down_j = lax.rem(j + 1, spans), lax.rem(j + spans - 1, spans)
    up_k, down_k = lax.rem(k + 1, depths), lax.rem(k + depths - 1, depths)
    is_bottom, is_top = k == 0, k == depths - 1
    mesh_id = pl.DeviceIdType.MESH

    def remote(src, dst, index, **where):
        return pltpu.make_async_remote_copy(
            src_ref=src,
            dst_ref=dst,
            send_sem=send_sem.at[index],
            recv_sem=recv_sem.at[index],
            device_id=where,
            device_id_type=mesh_id,
        )

    def local(src, dst, index):
        return pltpu.make_async_copy(src, dst, local_sem.at[index])

    barrier = pltpu.get_barrier_semaphore()
    for m in range(1, streams):
        pl.semaphore_signal(barrier, inc=1, device_id={"stream": lax.rem(i + m, streams)}, device_id_type=mesh_id)
    for other in (up_j, down_j):
        pl.semaphore_signal(barrier, inc=1, device_id={"span": other}, device_id_type=mesh_id)
    for m in range(1, depths):
        pl.semaphore_signal(barrier, inc=1, device_id={"depth": lax.rem(k + m, depths)}, device_id_type=mesh_id)

    load_t = local(t_in, tb.at[pl.ds(CELLS, ROWS * CELLS)], 0)
    load_v = local(v_in, vb.at[pl.ds(CELLS, ROWS * CELLS)], 1)
    load_c = local(c_in, xn.at[pl.ds(SWEEPS * LAYERS, ROWS * LAYERS)], 2)
    load_t.start()
    load_c.start()
    load_v.start()

    lane32 = lane_of((CELLS, LANES))
    load_t.wait()
    n_send[1] = tb[pl.ds(CELLS + CELLS - 1, ROWS, stride=CELLS), :]
    n_send[3] = tb[pl.ds(CELLS, ROWS, stride=CELLS), :]
    load_c.wait()
    surface[i] = xn[pl.ds(SWEEPS * LAYERS, ROWS, stride=LAYERS), :]
    load_v.wait()
    n_send[0] = vb[pl.ds(CELLS + CELLS - 1, ROWS, stride=CELLS), :]
    n_send[2] = vb[pl.ds(CELLS, ROWS, stride=CELLS), :]

    def pack_fluid(row, carry):
        right, left = carry
        at = pl.ds(pl.multiple_of(CELLS + row * CELLS, CELLS), CELLS)
        v, t = vb[at, :], tb[at, :]
        right = jnp.where(lane32 == row, roll(v, row + 1), right)
        right = jnp.where(lane32 == row + ROWS, roll(t, row + 1 + ROWS), right)
        left = jnp.where(lane32 == row, roll(v, row), left)
        left = jnp.where(lane32 == row + ROWS, roll(t, row + ROWS), left)
        return right, left

    zero32 = jnp.zeros((CELLS, LANES), jnp.float32)
    right, left = rows_loop(0, ROWS, 4, pack_fluid, (zero32, zero32))
    w_send[0] = right
    w_send[1] = left

    pl.semaphore_wait(barrier, streams - 1 + 2 + depths - 1)

    surfaces = [
        remote(surface.at[i], surface.at[i], GATHER + m, stream=lax.rem(i + m, streams))
        for m in range(1, streams)
    ]
    fluxes = [
        remote(flux.at[i], flux.at[i], GATHER + streams + m, stream=lax.rem(i + m, streams))
        for m in range(1, streams)
    ]
    walls = [
        remote(wall_send, wall_all.at[i], GATHER + 2 * streams + m, stream=lax.rem(i + m, streams))
        for m in range(1, streams)
    ]
    planes = [
        remote(n_send.at[3], t0_recv.at[0], T0_UP, span=up_j),
        remote(n_send.at[3], t0_recv.at[1], T0_DOWN, span=down_j),
    ]
    last, first = pl.ds(ROWS * CELLS, CELLS), pl.ds(CELLS, CELLS)
    before, after = pl.ds(0, CELLS), pl.ds((ROWS + 1) * CELLS, CELLS)
    t_halos = [
        remote(tb.at[last], tb.at[before], T_UP, stream=up_i),
        remote(tb.at[first], tb.at[after], T_DOWN, stream=down_i),
    ]
    v_halos = [
        remote(vb.at[last], vb.at[before], V_UP, stream=up_i),
        remote(vb.at[first], vb.at[after], V_DOWN, stream=down_i),
    ]
    n_halos = [
        remote(n_send.at[pl.ds(0, 2)], n_recv.at[pl.ds(0, 2)], N_UP, depth=up_k),
        remote(n_send.at[pl.ds(2, 2)], n_recv.at[pl.ds(2, 2)], N_DOWN, depth=down_k),
    ]
    w_halos = [
        remote(w_send.at[0], w_recv.at[0], W_UP, span=up_j),
        remote(w_send.at[1], w_recv.at[1], W_DOWN, span=down_j),
    ]
    wide = SWEEPS * LAYERS
    c_halos = [
        remote(xn.at[pl.ds(ROWS * LAYERS, wide)], xn.at[pl.ds(0, wide)], C_UP, stream=up_i),
        remote(xn.at[pl.ds(wide, wide)], xn.at[pl.ds(wide + ROWS * LAYERS, wide)], C_DOWN, stream=down_i),
    ]
    e_halos = [
        remote(e_send.at[0], e_recv.at[0], E_UP, span=up_j),
        remote(e_send.at[1], e_recv.at[1], E_DOWN, span=down_j),
    ]
    s_halos = [
        remote(source.at[0], source.at[1], S_UP, span=up_j),
        remote(source.at[0], source.at[2], S_DOWN, span=down_j),
    ]
    copies = [
        remote(source.at[0], source.at[0], GATHER + 3 * streams + m, depth=m) for m in range(1, depths)
    ]

    @pl.when(is_bottom)
    def _():
        for c in surfaces + planes:
            c.start()

    for c in t_halos + v_halos + w_halos + n_halos + c_halos:
        c.start()

    def arrange(row, carry):
        base = row * LAYERS
        for r in range(8):
            rm[row, r] = xn[pl.ds(base + r, 8, stride=8), :]
        return carry

    rows_loop(SWEEPS, SWEEPS + ROWS, 2, arrange, 0)

    for c in t_halos:
        c.wait_recv()

    @pl.when(is_bottom)
    def _():
        for c in surfaces + planes:
            c.wait_recv()
        sub = sub_of((ROWS, LANES))
        lane = lane_of((ROWS, LANES))
        face_temp = route(surface[...].reshape(streams * ROWS, LANES), shift_ref[...] + i * ROWS, ROWS)
        t0 = n_send[3]
        t1 = tb[pl.ds(CELLS + 1, ROWS, stride=CELLS), :]
        v0 = n_send[2]
        mask = mask_ref[...]
        behind = jnp.where(sub == 0, jnp.broadcast_to(tb[pl.ds(0, 1), :], (ROWS, LANES)), roll(t0, 1, 0))
        ahead = jnp.where(
            sub == ROWS - 1,
            jnp.broadcast_to(tb[pl.ds((ROWS + 1) * CELLS, 1), :], (ROWS, LANES)),
            roll(t0, ROWS - 1, 0),
        )
        west = jnp.where(lane == 0, roll(t0_recv[0], 1), roll(t0, 1))
        east = jnp.where(lane == LANES - 1, roll(t0_recv[1], LANES - 1), roll(t0, LANES - 1))
        under = jnp.where(mask > 0, face_temp, t0)
        lap = (ahead + behind) + (west + east) + (under + t1) - 6.0 * t0
        grad = (ahead - behind) * 0.5
        new = t0 + DIFFUSIVITY * lap - ADVECTION * v0 * grad
        flux[i] = mask.astype(jnp.float32) * TRANSFER * (new - face_temp)
        for c in fluxes:
            c.start()
        below[0] = -v0
        below[1] = under

    @pl.when(jnp.logical_not(is_bottom))
    def _():
        n_halos[0].wait_recv()
        below[0] = n_recv[0]
        below[1] = n_recv[1]

    @pl.when(is_bottom)
    def _():
        n_halos[0].wait_recv()

    for c in v_halos + w_halos + n_halos[1:]:
        c.wait_recv()

    sub32 = sub_of((CELLS, LANES))
    w_low, w_high = w_recv[0], w_recv[1]

    def fluid(row, carry):
        base = pl.multiple_of(row * CELLS, CELLS)
        here = pl.ds(base + CELLS, CELLS)
        velocity = vb[here, :]
        for field, (ref, out, coef) in enumerate(((vb, ov, VISCOSITY), (tb, ot, DIFFUSIVITY))):
            x = velocity if field == 0 else ref[here, :]
            behind = ref[pl.ds(base, CELLS), :]
            ahead = ref[pl.ds(base + 2 * CELLS, CELLS), :]
            at = row + field * ROWS
            west = jnp.where(lane32 == 0, roll(w_low, LANES - at), roll(x, 1))
            east = jnp.where(lane32 == LANES - 1, roll(w_high, LANES - 1 - at), roll(x, LANES - 1))
            under = jnp.broadcast_to(below[field, pl.ds(row, 1), :], (CELLS, LANES))
            over = jnp.where(is_top, x[CELLS - 1 :], n_recv[2 + field, pl.ds(row, 1), :])
            over = jnp.broadcast_to(over, (CELLS, LANES))
            lower = jnp.where(sub32 == 0, under, roll(x, 1, 0))
            upper = jnp.where(sub32 == CELLS - 1, over, roll(x, CELLS - 1, 0))
            lap = (ahead + behind) + (west + east) + (lower + upper) - 6.0 * x
            grad = (ahead - behind) * 0.5
            out[pl.ds(base, CELLS), :] = x + coef * lap - ADVECTION * velocity * grad
        return carry

    rows_loop(0, ROWS, 2, fluid, 0)
    store_v = local(ov, v_out, 3)
    store_t = local(ot, t_out, 4)
    store_v.start()
    store_t.start()

    for c in c_halos:
        c.wait_recv()
    rows_loop(0, SWEEPS, 2, arrange, 0)
    rows_loop(SWEEPS + ROWS, EXT, 2, arrange, 0)
    lane8 = lane_of((8, 8, LANES))

    for q in range(2):

        def pack_copper(n, carry):
            high, low = carry
            x = rm[1 + q * PACK + n]
            at = SWEEPS * n
            chosen = jnp.logical_and(lane8 >= at, lane8 < at + SWEEPS)
            high = jnp.where(chosen, roll(x, at + SWEEPS), high)
            low = jnp.where(chosen, roll(x, at), low)
            return high, low

        zero8 = jnp.zeros((8, 8, LANES), jnp.float32)
        high, low = rows_loop(0, PACK, 3, pack_copper, (zero8, zero8))
        e_send[0, q] = high
        e_send[1, q] = low
    for c in e_halos:
        c.start()

    def sweep_main(sweep):
        copper_sweep(xm, rm if sweep == 0 else xm, rm, 1 + sweep, EXT - 1 - sweep, sweep)

    sweep_main(0)

    @pl.when(is_bottom)
    def _():
        for c in fluxes:
            c.wait_recv()
        amount = i * ROWS - SWEEPS - shift_ref[...]
        source[0] = route(flux[...].reshape(streams * ROWS, LANES), amount, SOURCE_ROWS)
        for c in copies:
            c.start()

    sweep_main(1)
    sweep_main(2)

    for m in range(1, depths):

        @pl.when(k == m)
        def _():
            copies[m - 1].wait_recv()

    for c in s_halos:
        c.start()

    for sweep in range(3, SWEEPS):
        sweep_main(sweep)

    for c in e_halos:
        c.wait_recv()

    def build(row, carry):
        x0, x1 = rm[row], rm[row + HALF]
        f0 = jnp.maximum(row - 1, 0)
        f1 = jnp.minimum(row + HALF - 1, 2 * PACK - 1)
        q0, q1 = f0 // PACK, f1 // PACK
        p0, p1 = SWEEPS * (f0 - q0 * PACK), SWEEPS * (f1 - q1 * PACK)
        parts = (
            x0,
            roll(x0, 32),
            roll(e_recv[1, q0], lax.rem(LANES + 32 - p0, LANES)),
            roll(e_recv[0, q1], lax.rem(LANES + 58 - p1, LANES)),
            roll(x1, 64),
            roll(x1, 96),
            roll(e_recv[1, q1], lax.rem(LANES + 96 - p1, LANES)),
            roll(e_recv[0, q0], lax.rem(LANES + 122 - p0, LANES)),
        )
        rs[row] = regions(lane8, parts)
        return carry

    lax.fori_loop(0, STRIP, build, 0)
    for sweep in range(SWEEPS):
        copper_sweep(xs, rs if sweep == 0 else xs, rs, 1 + sweep, STRIP - 1 - sweep, sweep)

    for half in range(2):

        def assemble(n, carry):
            done = with_edges(lane8, xm[n + SWEEPS + half * HALF], xs[n + SWEEPS], half)
            base = (n + half * HALF) * LAYERS
            for r in range(8):
                oc[pl.ds(base + r, 8, stride=8), :] = done[r]
            return carry

        rows_loop(0, HALF, 2, assemble, 0)

    for c in s_halos:
        c.wait_recv()
    lane = lane_of((32, LANES))
    low0, low1 = source[0, pl.ds(0, 32), :], source[0, pl.ds(HALF, 32), :]
    strip_source[...] = regions(
        lane,
        (
            low0,
            roll(low0, 32),
            roll(source[2, pl.ds(0, 32), :], 32),
            roll(source[1, pl.ds(HALF, 32), :], 64),
            roll(low1, 64),
            roll(low1, 96),
            roll(source[2, pl.ds(HALF, 32), :], 96),
            source[1, pl.ds(0, 32), :],
        ),
    )
    for sweep in range(SWEEPS):
        source_sweep(gm, source.at[0], 1 + sweep, EXT - 1 - sweep, sweep)
        source_sweep(gs, strip_source, 1 + sweep, STRIP - 1 - sweep, sweep)
    lane1 = lane_of((8, LANES))
    for half in range(2):

        def add(n, carry):
            at = pl.ds(pl.multiple_of((n + half * HALF) * LAYERS, LAYERS), 8)
            oc[at, :] += with_edges(lane1, gm[n + SWEEPS + half * HALF], gs[n + SWEEPS], half)
            return carry

        rows_loop(0, HALF, 8, add, 0)

    columns = LANES // depths
    tiles = ROWS // 8
    new_surface = oc[pl.ds(0, ROWS, stride=LAYERS), :]
    packed = jnp.zeros((8, LANES), jnp.float32)
    width = LANES // tiles
    for t in range(tiles):
        moved = roll(new_surface[8 * t : 8 * t + 8], lax.rem(LANES + width * t - columns * k, LANES))
        packed = jnp.where(lane1 // width == t, moved, packed)
    wall_send[...] = packed
    for c in walls:
        c.start()
    store_c = local(oc, c_out, 5)
    store_c.start()
    wall_all[i] = packed
    shift = roll(jnp.broadcast_to(shift_ref[...], (8, LANES)), lax.rem(LANES - columns * k, LANES))[:1]
    for c in walls:
        c.wait_recv()
    rows = [roll(wall_all[b], LANES - width * t) for b in range(streams) for t in range(tiles)]
    wall_ref[...] = route(jnp.concatenate(rows, axis=0), shift + i * ROWS, ROWS)[:, : wall_ref.shape[1]]

    for c in t_halos + v_halos + w_halos + n_halos + c_halos + e_halos + s_halos + walls:
        c.wait_send()

    @pl.when(is_bottom)
    def _():
        for c in surfaces + planes + fluxes + copies:
            c.wait_send()

    store_v.wait()
    store_t.wait()
    store_c.wait()


def per_device(fluid_velocity, fluid_temp, solid_temp, channel_mask, owner_shift):
    f32 = jnp.float32
    streams, depths = lax.axis_size("stream"), lax.axis_size("depth")
    fluid_rows, copper_rows = ROWS * CELLS, ROWS * LAYERS
    vmem = pl.BlockSpec(memory_space=pltpu.VMEM)
    anywhere = pl.BlockSpec(memory_space=pl.ANY)
    messages = GATHER + 3 * streams + depths
    outs = pl.pallas_call(
        kernel,
        out_shape=(
            jax.ShapeDtypeStruct((fluid_rows, LANES), f32),
            jax.ShapeDtypeStruct((fluid_rows, LANES), f32),
            jax.ShapeDtypeStruct((copper_rows, LANES), f32),
            jax.ShapeDtypeStruct((ROWS, LANES // depths), f32),
        ),
        in_specs=[anywhere, anywhere, anywhere, vmem, vmem],
        out_specs=(anywhere, anywhere, anywhere, vmem),
        scratch_shapes=[
            pltpu.VMEM(((ROWS + 2) * CELLS, LANES), f32),
            pltpu.VMEM(((ROWS + 2) * CELLS, LANES), f32),
            pltpu.VMEM((EXT * LAYERS, LANES), f32),
            pltpu.VMEM((EXT, 8, 8, LANES), f32),
            pltpu.VMEM((EXT, 8, 8, LANES), f32),
            pltpu.VMEM((STRIP, 8, 8, LANES), f32),
            pltpu.VMEM((STRIP, 8, 8, LANES), f32),
            pltpu.VMEM((copper_rows, LANES), f32),
            pltpu.VMEM((fluid_rows, LANES), f32),
            pltpu.VMEM((fluid_rows, LANES), f32),
            pltpu.VMEM((4, ROWS, LANES), f32),
            pltpu.VMEM((4, ROWS, LANES), f32),
            pltpu.VMEM((2, CELLS, LANES), f32),
            pltpu.VMEM((2, CELLS, LANES), f32),
            pltpu.VMEM((2, ROWS, LANES), f32),
            pltpu.VMEM((2, 2, 8, 8, LANES), f32),
            pltpu.VMEM((2, 2, 8, 8, LANES), f32),
            pltpu.VMEM((streams, ROWS, LANES), f32),
            pltpu.VMEM((streams, ROWS, LANES), f32),
            pltpu.VMEM((ROWS, LANES), f32),
            pltpu.VMEM((3, SOURCE_ROWS, LANES), f32),
            pltpu.VMEM((32, LANES), f32),
            pltpu.VMEM((EXT, 8, LANES), f32),
            pltpu.VMEM((STRIP, 8, LANES), f32),
            pltpu.VMEM((8, LANES), f32),
            pltpu.VMEM((streams, 8, LANES), f32),
            pltpu.VMEM((2, ROWS, LANES), f32),
            pltpu.SemaphoreType.DMA((messages,)),
            pltpu.SemaphoreType.DMA((messages,)),
            pltpu.SemaphoreType.DMA((6,)),
        ],
        compiler_params=pltpu.CompilerParams(
            collective_id=0, has_side_effects=True, vmem_limit_bytes=40 * 1024 * 1024
        ),
    )(
        fluid_velocity.reshape(fluid_rows, LANES),
        fluid_temp.reshape(fluid_rows, LANES),
        solid_temp.reshape(copper_rows, LANES),
        channel_mask,
        owner_shift.reshape(1, LANES),
    )
    return (
        outs[0].reshape(fluid_velocity.shape),
        outs[1].reshape(fluid_temp.shape),
        outs[2].reshape(solid_temp.shape),
        outs[3],
    )


def solution(mesh):
    placed = (
        P("stream", "depth", "span"),
        P("stream", "depth", "span"),
        P("stream", None, "span"),
        P("stream", "span"),
        P("span"),
    )
    return jax.shard_map(
        per_device,
        mesh=mesh,
        in_specs=placed,
        out_specs=(
            P("stream", "depth", "span"),
            P("stream", "depth", "span"),
            P("stream", None, "span"),
            P("stream", ("span", "depth")),
        ),
        check_vma=False,
    )
```

profile of v0, /device:TPU:0, one launch (start us, length us, event | category | flops | bytes accessed | tf_op | source)
XLA Modules:
  0.0 58.0 jit_solution(5176078739156113577)
XLA Ops:
  0.6 0.0 copy-start.4
  0.6 0.6 %copy-done.4 = s32[128]{0:T(128)S(1)} copy-done((s32[128]{0:T(128)S(1)}, s32[128]{0:T(128)}, u32[]{:S(2)}) %copy-start.4) | copy-done | bytes 536
  1.3 0.0 copy-start
  1.3 1.2 %copy-done = f32[32,64,128]{2,1,0:T(8,128)S(1)} copy-done((f32[32,64,128]{2,1,0:T(8,128)S(1)}, f32[32,64,128]{2,1,0:T(8,128)}, u32[]{:S(2)}) %copy-start) | copy-done | bytes 1048600
  2.5 0.0 copy-start.1
  2.5 1.0 %copy-done.1 = f32[32,32,128]{2,1,0:T(8,128)S(1)} copy-done((f32[32,32,128]{2,1,0:T(8,128)S(1)}, f32[32,32,128]{2,1,0:T(8,128)}, u32[]{:S(2)}) %copy-start.1) | copy-done | bytes 524312
  3.6 0.0 copy-start.2
  3.6 1.0 %copy-done.2 = f32[32,32,128]{2,1,0:T(8,128)S(1)} copy-done((f32[32,32,128]{2,1,0:T(8,128)S(1)}, f32[32,32,128]{2,1,0:T(8,128)}, u32[]{:S(2)}) %copy-start.2) | copy-done | bytes 524312
  4.6 0.0 copy-start.3
  4.6 0.7 %copy-done.3 = s32[32,128]{1,0:T(8,128)S(1)} copy-done((s32[32,128]{1,0:T(8,128)S(1)}, s32[32,128]{1,0:T(8,128)}, u32[]{:S(2)}) %copy-start.3) | copy-done | bytes 16408
  5.3 49.5 %shard_map.84 = (f32[1024,128]{1,0:T(8,128)S(1)}, f32[1024,128]{1,0:T(8,128)S(1)}, f32[2048,128]{1,0:T(8,128)S(1)}, f32[32,32]{1,0:T(8,128)S(1)}) custom-call(f32[1024,128]{1,0:T(8,128)S(1)} %bitcast.9, f32[1024,128]{1,0:T(8,128)S(1)} %bitcast.10, f32[2048,128]{1,0:T(8,128)S(1)} %bitcast.7, s32[32,128]{1,0:T(8,128)S(1)} %copy-done.3, s32[1,128]{1,0:T(1,128)S(1)} %bitcast.13), custom_call_target="tpu_custom_call" | custom-call | tf_op jit(solution)/shard_map/pallas_call | solution.py:560
  54.8 0.8 %copy.13 = f32[32,32,128]{2,1,0:T(8,128)} copy(f32[32,32,128]{2,1,0:T(8,128)S(1)} %bitcast.12) | data formatting | bytes 1048576
  55.6 0.8 %copy.14 = f32[32,32,128]{2,1,0:T(8,128)} copy(f32[32,32,128]{2,1,0:T(8,128)S(1)} %bitcast.11) | data formatting | bytes 1048576
  56.4 1.0 %copy.15 = f32[32,64,128]{2,1,0:T(8,128)} copy(f32[32,64,128]{2,1,0:T(8,128)S(1)} %bitcast.8) | data formatting | bytes 2097152
  57.4 0.6 %copy.16 = f32[32,32]{1,0:T(8,128)} copy(f32[32,32]{1,0:T(8,128)S(1)} %get-tuple-element.19) | data formatting | bytes 8192
Async XLA Ops:
  0.6 0.7 %copy-start.4 = (s32[128]{0:T(128)S(1)}, s32[128]{0:T(128)}, u32[]{:S(2)}) copy-start(s32[128]{0:T(128)} %param.9) | copy-start | bytes 1540
  1.3 1.2 %copy-start = (f32[32,64,128]{2,1,0:T(8,128)S(1)}, f32[32,64,128]{2,1,0:T(8,128)}, u32[]{:S(2)}) copy-start(f32[32,64,128]{2,1,0:T(8,128)} %param.7) | copy-start | bytes 3145732
  2.5 1.0 %copy-start.1 = (f32[32,32,128]{2,1,0:T(8,128)S(1)}, f32[32,32,128]{2,1,0:T(8,128)}, u32[]{:S(2)}) copy-start(f32[32,32,128]{2,1,0:T(8,128)} %param.5) | copy-start | bytes 1572868
  3.6 1.0 %copy-start.2 = (f32[32,32,128]{2,1,0:T(8,128)S(1)}, f32[32,32,128]{2,1,0:T(8,128)}, u32[]{:S(2)}) copy-start(f32[32,32,128]{2,1,0:T(8,128)} %param.6) | copy-start | bytes 1572868
  4.6 0.7 %copy-start.3 = (s32[32,128]{1,0:T(8,128)S(1)}, s32[32,128]{1,0:T(8,128)}, u32[]{:S(2)}) copy-start(s32[32,128]{1,0:T(8,128)} %mask_ref.1) | copy-start | bytes 49156
where the time goes:
time: 58.3 us; the launch traced here: 58 us
  Pallas kernels  49.5 us (85%)
  local copies, waits for them, and re-layouts  7.83 us (13%)
  between operations  0.65 us (1%)
    pallas_call x1, Pallas kernels, per_device(): pl.pallas_call(kernel, out_shape=(jax.ShapeDtypeStruct((fluid_rows, LANES...  49.5 us
    unnamed x14, local copies, waits for them, and re-layouts  7.83 us

commit v1 on v0

--- a/solution.py
+++ b/solution.py
@@ -21,7 +21,8 @@
 EXT = ROWS + 2 * SWEEPS
 HALF = ROWS // 2
 STRIP = HALF + 2 * SWEEPS
-PACK = 21
+PACK = 10
+GROUPS = 3
 SOURCE_ROWS = 48
 
 V_UP, V_DOWN, T_UP, T_DOWN = 0, 1, 2, 3
@@ -113,42 +114,13 @@
         out[row] = keep * cur + gain * (rhs[row] + near)
         return cur, nxt
 
-    rows_loop(first, last, 2, body, (src[first - 1], src[first]))
-
-
-def source_sweep(state, source, first, last, sweep):
-    omega = weight(sweep)
-    keep, gain = 1.0 - omega, omega / 7.0
-    sub = sub_of((8, LANES))
-
-    def fed(row):
-        return jnp.where(sub == 0, jnp.broadcast_to(source[pl.ds(row, 1), :], (8, LANES)), 0.0)
-
-    if sweep == 0:
-
-        def begin(row, carry):
-            state[row] = gain * fed(row)
-            return carry
-
-        rows_loop(first, last, 6, begin, 0)
-        return
-
-    def body(row, carry):
-        prev, cur = carry
-        nxt = state[row + 1]
-        side = roll(cur, 1) + roll(cur, LANES - 1)
-        up = jnp.where(sub == 7, 0.0, roll(cur, 7, 0))
-        down = jnp.where(sub == 0, cur, roll(cur, 1, 0))
-        near = (prev + nxt) + (up + down) + side
-        state[row] = keep * cur + gain * (fed(row) + near)
-        return cur, nxt
-
-    rows_loop(first, last, 8, body, (state[first - 1], state[first]))
-
-
-def with_edges(lane, main, strip, half):
-    low, high = (roll(strip, 0), roll(strip, 96)) if half == 0 else (roll(strip, 64), roll(strip, 32))
-    return jnp.where(lane < SWEEPS, low, jnp.where(lane >= LANES - SWEEPS, high, main))
+    rows_loop(first, last, (last - first) // 2, body, (src[first - 1], src[first]))
+
+
+def edge_index(row):
+    n = lax.rem(row + STRIP - SWEEPS, STRIP)
+    group = n // PACK
+    return group, SWEEPS * (n - group * PACK)
 
 
 def kernel(
@@ -165,12 +137,11 @@
     tb,
     xn,
     rm,
-    xm,
+    x0,
+    x1,
     rs,
-    xs,
-    oc,
-    ov,
-    ot,
+    s0,
+    s1,
     n_send,
     n_recv,
     w_send,
@@ -180,11 +151,9 @@
     e_recv,
     surface,
     flux,
-    face,
     source,
+    fix,
     strip_source,
-    gm,
-    gs,
     wall_send,
     wall_all,
     below,
@@ -238,20 +207,15 @@
     n_send[0] = vb[pl.ds(CELLS + CELLS - 1, ROWS, stride=CELLS), :]
     n_send[2] = vb[pl.ds(CELLS, ROWS, stride=CELLS), :]
 
-    def pack_fluid(row, carry):
-        right, left = carry
+    def pack_fluid(row, packed):
         at = pl.ds(pl.multiple_of(CELLS + row * CELLS, CELLS), CELLS)
-        v, t = vb[at, :], tb[at, :]
-        right = jnp.where(lane32 == row, roll(v, row + 1), right)
-        right = jnp.where(lane32 == row + ROWS, roll(t, row + 1 + ROWS), right)
-        left = jnp.where(lane32 == row, roll(v, row), left)
-        left = jnp.where(lane32 == row + ROWS, roll(t, row + ROWS), left)
-        return right, left
-
-    zero32 = jnp.zeros((CELLS, LANES), jnp.float32)
-    right, left = rows_loop(0, ROWS, 4, pack_fluid, (zero32, zero32))
-    w_send[0] = right
-    w_send[1] = left
+        low = 2 * row
+        for ref, place in ((vb, low), (tb, low + 64)):
+            chosen = jnp.logical_or(lane32 == place, lane32 == ((place + LANES - 1) & (LANES - 1)))
+            packed = jnp.where(chosen, roll(ref[at, :], place), packed)
+        return packed
+
+    w_send[...] = rows_loop(0, ROWS, 8, pack_fluid, jnp.zeros((CELLS, LANES), jnp.float32))
 
     pl.semaphore_wait(barrier, streams - 1 + 2 + depths - 1)
 
@@ -286,8 +250,8 @@
         remote(n_send.at[pl.ds(2, 2)], n_recv.at[pl.ds(2, 2)], N_DOWN, depth=down_k),
     ]
     w_halos = [
-        remote(w_send.at[0], w_recv.at[0], W_UP, span=up_j),
-        remote(w_send.at[1], w_recv.at[1], W_DOWN, span=down_j),
+        remote(w_send, w_recv.at[0], W_UP, span=up_j),
+        remote(w_send, w_recv.at[1], W_DOWN, span=down_j),
     ]
     wide = SWEEPS * LAYERS
     c_halos = [
@@ -320,7 +284,30 @@
             rm[row, r] = xn[pl.ds(base + r, 8, stride=8), :]
         return carry
 
-    rows_loop(SWEEPS, SWEEPS + ROWS, 2, arrange, 0)
+    rows_loop(SWEEPS, SWEEPS + ROWS, 4, arrange, 0)
+
+    lane8 = lane_of((8, 8, LANES))
+    part = (lane8 & 63) // 16
+    outer = jnp.logical_or(lane8 < 32, lane8 >= 96)
+
+    def edges(row, place, carry):
+        high, low = carry
+        ends = jnp.where(outer, rm[row], roll(rm[row + HALF], 64))
+        rs[row] = jnp.where(part == 1, roll(ends, 32), ends)
+        chosen = jnp.logical_and((lane8 & 63) >= place, (lane8 & 63) < place + SWEEPS)
+        return (
+            jnp.where(chosen, roll(ends, place + SWEEPS), high),
+            jnp.where(chosen, roll(ends, place), low),
+        )
+
+    zero8 = jnp.zeros((8, 8, LANES), jnp.float32)
+
+    def edge_run(first, last, start, carry):
+        return rows_loop(first, last, 2, lambda row, c: edges(row, SWEEPS * (row - start), c), carry)
+
+    e_send[0, 0], e_send[1, 0] = edge_run(SWEEPS, SWEEPS + PACK, SWEEPS, (zero8, zero8))
+    middle = SWEEPS + PACK
+    e_send[0, 1], e_send[1, 1] = edge_run(middle, HALF + SWEEPS, middle, (zero8, zero8))
 
     for c in t_halos:
         c.wait_recv()
@@ -368,19 +355,19 @@
         c.wait_recv()
 
     sub32 = sub_of((CELLS, LANES))
-    w_low, w_high = w_recv[0], w_recv[1]
+    w_all = jnp.where((lane32 & 1) == 0, roll(w_recv[0], 1), roll(w_recv[1], LANES - 1))
 
     def fluid(row, carry):
         base = pl.multiple_of(row * CELLS, CELLS)
         here = pl.ds(base + CELLS, CELLS)
         velocity = vb[here, :]
-        for field, (ref, out, coef) in enumerate(((vb, ov, VISCOSITY), (tb, ot, DIFFUSIVITY))):
+        for field, (ref, out, coef) in enumerate(((vb, v_out, VISCOSITY), (tb, t_out, DIFFUSIVITY))):
             x = velocity if field == 0 else ref[here, :]
             behind = ref[pl.ds(base, CELLS), :]
             ahead = ref[pl.ds(base + 2 * CELLS, CELLS), :]
-            at = row + field * ROWS
-            west = jnp.where(lane32 == 0, roll(w_low, LANES - at), roll(x, 1))
-            east = jnp.where(lane32 == LANES - 1, roll(w_high, LANES - 1 - at), roll(x, LANES - 1))
+            ends = roll(w_all, lax.rem(LANES - 2 * row, LANES) if field == 0 else 64 - 2 * row)
+            west = jnp.where(lane32 == 0, ends, roll(x, 1))
+            east = jnp.where(lane32 == LANES - 1, ends, roll(x, LANES - 1))
             under = jnp.broadcast_to(below[field, pl.ds(row, 1), :], (CELLS, LANES))
             over = jnp.where(is_top, x[CELLS - 1 :], n_recv[2 + field, pl.ds(row, 1), :])
             over = jnp.broadcast_to(over, (CELLS, LANES))
@@ -391,40 +378,19 @@
             out[pl.ds(base, CELLS), :] = x + coef * lap - ADVECTION * velocity * grad
         return carry
 
-    rows_loop(0, ROWS, 2, fluid, 0)
-    store_v = local(ov, v_out, 3)
-    store_t = local(ot, t_out, 4)
-    store_v.start()
-    store_t.start()
+    rows_loop(0, ROWS, 8, fluid, 0)
 
     for c in c_halos:
         c.wait_recv()
-    rows_loop(0, SWEEPS, 2, arrange, 0)
-    rows_loop(SWEEPS + ROWS, EXT, 2, arrange, 0)
-    lane8 = lane_of((8, 8, LANES))
-
-    for q in range(2):
-
-        def pack_copper(n, carry):
-            high, low = carry
-            x = rm[1 + q * PACK + n]
-            at = SWEEPS * n
-            chosen = jnp.logical_and(lane8 >= at, lane8 < at + SWEEPS)
-            high = jnp.where(chosen, roll(x, at + SWEEPS), high)
-            low = jnp.where(chosen, roll(x, at), low)
-            return high, low
-
-        zero8 = jnp.zeros((8, 8, LANES), jnp.float32)
-        high, low = rows_loop(0, PACK, 3, pack_copper, (zero8, zero8))
-        e_send[0, q] = high
-        e_send[1, q] = low
+    rows_loop(0, SWEEPS, 6, arrange, 0)
+    rows_loop(SWEEPS + ROWS, EXT, 6, arrange, 0)
+    carry = edge_run(HALF + SWEEPS, middle + PACK, middle, (e_send[0, 1], e_send[1, 1]))
+    e_send[0, 1], e_send[1, 1] = carry
+    carry = edge_run(middle + PACK, STRIP, middle + PACK, (zero8, zero8))
+    carry = edge_run(0, SWEEPS, middle + PACK - STRIP, carry)
+    e_send[0, 2], e_send[1, 2] = carry
     for c in e_halos:
         c.start()
-
-    def sweep_main(sweep):
-        copper_sweep(xm, rm if sweep == 0 else xm, rm, 1 + sweep, EXT - 1 - sweep, sweep)
-
-    sweep_main(0)
 
     @pl.when(is_bottom)
     def _():
@@ -435,8 +401,12 @@
         for c in copies:
             c.start()
 
+    def sweep_main(sweep):
+        a, b = (x0, x1) if sweep % 2 == 0 else (x1, x0)
+        copper_sweep(a, rm if sweep == 0 else b, rm, 1 + sweep, EXT - 1 - sweep, sweep)
+
+    sweep_main(0)
     sweep_main(1)
-    sweep_main(2)
 
     for m in range(1, depths):
 
@@ -447,46 +417,39 @@
     for c in s_halos:
         c.start()
 
-    for sweep in range(3, SWEEPS):
+    heat = source[0]
+    gains = [weight(n) / 7.0 for n in range(2)]
+    once = gains[0] * heat
+    near = roll(once, 1, 0) + roll(once, SOURCE_ROWS - 1, 0) + roll(once, 1) + roll(once, LANES - 1) + once
+    fix[0] = (1.0 - weight(1)) * once + gains[1] * (heat + near)
+    fix[1] = gains[1] * once
+    top = sub_of((8, LANES)) == 0
+
+    def top_row(ref, row):
+        return jnp.where(top, jnp.broadcast_to(ref[pl.ds(row, 1), :], (8, LANES)), 0.0)
+
+    def mend(row, carry):
+        rm[row, 0] += top_row(source.at[0], row)
+        x1[row, 0] += top_row(fix.at[0], row)
+        x1[row, 1] += top_row(fix.at[1], row)
+        return carry
+
+    rows_loop(2, EXT - 2, 8, mend, 0)
+    for sweep in range(2, SWEEPS):
         sweep_main(sweep)
 
     for c in e_halos:
         c.wait_recv()
 
     def build(row, carry):
-        x0, x1 = rm[row], rm[row + HALF]
-        f0 = jnp.maximum(row - 1, 0)
-        f1 = jnp.minimum(row + HALF - 1, 2 * PACK - 1)
-        q0, q1 = f0 // PACK, f1 // PACK
-        p0, p1 = SWEEPS * (f0 - q0 * PACK), SWEEPS * (f1 - q1 * PACK)
-        parts = (
-            x0,
-            roll(x0, 32),
-            roll(e_recv[1, q0], lax.rem(LANES + 32 - p0, LANES)),
-            roll(e_recv[0, q1], lax.rem(LANES + 58 - p1, LANES)),
-            roll(x1, 64),
-            roll(x1, 96),
-            roll(e_recv[1, q1], lax.rem(LANES + 96 - p1, LANES)),
-            roll(e_recv[0, q0], lax.rem(LANES + 122 - p0, LANES)),
-        )
-        rs[row] = regions(lane8, parts)
+        group, place = edge_index(row)
+        east = roll(e_recv[1, group], lax.rem(LANES + 32 - place, LANES))
+        west = roll(e_recv[0, group], 122 - place)
+        rs[row] = jnp.where(part == 2, east, jnp.where(part == 3, west, rs[row]))
         return carry
 
-    lax.fori_loop(0, STRIP, build, 0)
-    for sweep in range(SWEEPS):
-        copper_sweep(xs, rs if sweep == 0 else xs, rs, 1 + sweep, STRIP - 1 - sweep, sweep)
-
-    for half in range(2):
-
-        def assemble(n, carry):
-            done = with_edges(lane8, xm[n + SWEEPS + half * HALF], xs[n + SWEEPS], half)
-            base = (n + half * HALF) * LAYERS
-            for r in range(8):
-                oc[pl.ds(base + r, 8, stride=8), :] = done[r]
-            return carry
-
-        rows_loop(0, HALF, 2, assemble, 0)
-
+    rows_loop(0, STRIP, 4, build, 0)
+    copper_sweep(s0, rs, rs, 1, STRIP - 1, 0)
     for c in s_halos:
         c.wait_recv()
     lane = lane_of((32, LANES))
@@ -504,22 +467,41 @@
             source[1, pl.ds(0, 32), :],
         ),
     )
-    for sweep in range(SWEEPS):
-        source_sweep(gm, source.at[0], 1 + sweep, EXT - 1 - sweep, sweep)
-        source_sweep(gs, strip_source, 1 + sweep, STRIP - 1 - sweep, sweep)
+
+    def mend_strip(row, carry):
+        extra = top_row(strip_source, row)
+        rs[row, 0] += extra
+        s0[row, 0] += gains[0] * extra
+        return carry
+
+    rows_loop(1, STRIP - 1, 13, mend_strip, 0)
+    for sweep in range(1, SWEEPS):
+        a, b = (s0, s1) if sweep % 2 == 0 else (s1, s0)
+        copper_sweep(a, b, rs, 1 + sweep, STRIP - 1 - sweep, sweep)
+
+    def merged(lanes, main0, main1, strip):
+        high = roll(strip, 96)
+        other = roll(jnp.where(lanes < 64, high, strip), 64)
+        return tuple(
+            jnp.where(lanes < SWEEPS, low, jnp.where(lanes >= LANES - SWEEPS, up, main))
+            for low, up, main in ((strip, high, main0), (other, other, main1))
+        )
+
     lane1 = lane_of((8, LANES))
-    for half in range(2):
-
-        def add(n, carry):
-            at = pl.ds(pl.multiple_of((n + half * HALF) * LAYERS, LAYERS), 8)
-            oc[at, :] += with_edges(lane1, gm[n + SWEEPS + half * HALF], gs[n + SWEEPS], half)
-            return carry
-
-        rows_loop(0, HALF, 8, add, 0)
+
+    def assemble(n, carry):
+        halves = merged(lane8, x1[n + SWEEPS], x1[n + SWEEPS + HALF], s1[n + SWEEPS])
+        for half, done in enumerate(halves):
+            base = (n + half * HALF) * LAYERS
+            for r in range(8):
+                c_out[pl.ds(base + r, 8, stride=8), :] = done[r]
+        return carry
+
+    rows_loop(0, HALF, 4, assemble, 0)
 
     columns = LANES // depths
     tiles = ROWS // 8
-    new_surface = oc[pl.ds(0, ROWS, stride=LAYERS), :]
+    new_surface = c_out[pl.ds(0, ROWS, stride=LAYERS), :]
     packed = jnp.zeros((8, LANES), jnp.float32)
     width = LANES // tiles
     for t in range(tiles):
@@ -528,8 +510,6 @@
     wall_send[...] = packed
     for c in walls:
         c.start()
-    store_c = local(oc, c_out, 5)
-    store_c.start()
     wall_all[i] = packed
     shift = roll(jnp.broadcast_to(shift_ref[...], (8, LANES)), lax.rem(LANES - columns * k, LANES))[:1]
     for c in walls:
@@ -545,9 +525,17 @@
         for c in surfaces + planes + fluxes + copies:
             c.wait_send()
 
-    store_v.wait()
-    store_t.wait()
-    store_c.wait()
+
+def write_out(*refs):
+    *sources, semaphores = refs
+    count = len(sources) // 2
+    copies = [
+        pltpu.make_async_copy(sources[n], sources[count + n], semaphores.at[n]) for n in range(count)
+    ]
+    for c in copies:
+        c.start()
+    for c in copies:
+        c.wait()
 
 
 def per_device(fluid_velocity, fluid_temp, solid_temp, channel_mask, owner_shift):
@@ -556,6 +544,7 @@
     fluid_rows, copper_rows = ROWS * CELLS, ROWS * LAYERS
     vmem = pl.BlockSpec(memory_space=pltpu.VMEM)
     anywhere = pl.BlockSpec(memory_space=pl.ANY)
+    hbm = pl.BlockSpec(memory_space=pltpu.HBM)
     messages = GATHER + 3 * streams + depths
     outs = pl.pallas_call(
         kernel,
@@ -565,42 +554,35 @@
             jax.ShapeDtypeStruct((copper_rows, LANES), f32),
             jax.ShapeDtypeStruct((ROWS, LANES // depths), f32),
         ),
-        in_specs=[anywhere, anywhere, anywhere, vmem, vmem],
-        out_specs=(anywhere, anywhere, anywhere, vmem),
+        in_specs=[hbm, hbm, hbm, vmem, vmem],
+        out_specs=(vmem, vmem, vmem, vmem),
         scratch_shapes=[
             pltpu.VMEM(((ROWS + 2) * CELLS, LANES), f32),
             pltpu.VMEM(((ROWS + 2) * CELLS, LANES), f32),
             pltpu.VMEM((EXT * LAYERS, LANES), f32),
-            pltpu.VMEM((EXT, 8, 8, LANES), f32),
-            pltpu.VMEM((EXT, 8, 8, LANES), f32),
-            pltpu.VMEM((STRIP, 8, 8, LANES), f32),
-            pltpu.VMEM((STRIP, 8, 8, LANES), f32),
-            pltpu.VMEM((copper_rows, LANES), f32),
-            pltpu.VMEM((fluid_rows, LANES), f32),
-            pltpu.VMEM((fluid_rows, LANES), f32),
+            *[pltpu.VMEM((EXT, 8, 8, LANES), f32)] * 3,
+            *[pltpu.VMEM((STRIP, 8, 8, LANES), f32)] * 3,
             pltpu.VMEM((4, ROWS, LANES), f32),
             pltpu.VMEM((4, ROWS, LANES), f32),
-            pltpu.VMEM((2, CELLS, LANES), f32),
+            pltpu.VMEM((CELLS, LANES), f32),
             pltpu.VMEM((2, CELLS, LANES), f32),
             pltpu.VMEM((2, ROWS, LANES), f32),
-            pltpu.VMEM((2, 2, 8, 8, LANES), f32),
-            pltpu.VMEM((2, 2, 8, 8, LANES), f32),
+            pltpu.VMEM((2, GROUPS, 8, 8, LANES), f32),
+            pltpu.VMEM((2, GROUPS, 8, 8, LANES), f32),
             pltpu.VMEM((streams, ROWS, LANES), f32),
             pltpu.VMEM((streams, ROWS, LANES), f32),
-            pltpu.VMEM((ROWS, LANES), f32),
             pltpu.VMEM((3, SOURCE_ROWS, LANES), f32),
+            pltpu.VMEM((2, SOURCE_ROWS, LANES), f32),
             pltpu.VMEM((32, LANES), f32),
-            pltpu.VMEM((EXT, 8, LANES), f32),
-            pltpu.VMEM((STRIP, 8, LANES), f32),
             pltpu.VMEM((8, LANES), f32),
             pltpu.VMEM((streams, 8, LANES), f32),
             pltpu.VMEM((2, ROWS, LANES), f32),
             pltpu.SemaphoreType.DMA((messages,)),
             pltpu.SemaphoreType.DMA((messages,)),
-            pltpu.SemaphoreType.DMA((6,)),
+            pltpu.SemaphoreType.DMA((3,)),
         ],
         compiler_params=pltpu.CompilerParams(
-            collective_id=0, has_side_effects=True, vmem_limit_bytes=40 * 1024 * 1024
+            collective_id=0, has_side_effects=True, vmem_limit_bytes=24 * 1024 * 1024
         ),
     )(
         fluid_velocity.reshape(fluid_rows, LANES),
@@ -609,6 +591,14 @@
         channel_mask,
         owner_shift.reshape(1, LANES),
     )
+    outs = pl.pallas_call(
+        write_out,
+        out_shape=tuple(jax.ShapeDtypeStruct(o.shape, o.dtype) for o in outs),
+        in_specs=[anywhere] * 4,
+        out_specs=(anywhere,) * 4,
+        scratch_shapes=[pltpu.SemaphoreType.DMA((4,))],
+        compiler_params=pltpu.CompilerParams(vmem_limit_bytes=1024 * 1024),
+    )(*outs)
     return (
         outs[0].reshape(fluid_velocity.shape),
         outs[1].reshape(fluid_temp.shape),

time: 58.3 us -> 39.5 us (0.68)
  the two profiles are of different devices: /device:TPU:0 before, /device:TPU:4 now
where the time goes in v1:
time: 39.5 us; the launch traced here: 39.2 us
  Pallas kernels  33.9 us (86%)
  local copies, waits for them, and re-layouts  4.67 us (12%)
  between operations  0.65 us (2%)
    pallas_call x1, Pallas kernels, per_device(): pl.pallas_call(kernel, out_shape=(jax.ShapeDtypeStruct((fluid_rows, LANES...  32.5 us
    unnamed x10, local copies, waits for them, and re-layouts  4.67 us
    pallas_call x1, Pallas kernels, per_device(): pl.pallas_call(write_out, out_shape=tuple((jax.ShapeDtypeStruct(o.shape,...  1.35 us

profile of v1, /device:TPU:4, one launch (start us, length us, event | category | flops | bytes accessed | tf_op | source)
XLA Modules:
  0.0 39.2 jit_solution(15859808664982621578)
XLA Ops:
  0.6 0.0 copy-start.4
  0.6 0.6 %copy-done.4 = s32[128]{0:T(128)S(1)} copy-done((s32[128]{0:T(128)S(1)}, s32[128]{0:T(128)}, u32[]{:S(2)}) %copy-start.4) | copy-done | bytes 536
  1.3 0.0 copy-start
  1.3 1.2 %copy-done = f32[32,64,128]{2,1,0:T(8,128)S(1)} copy-done((f32[32,64,128]{2,1,0:T(8,128)S(1)}, f32[32,64,128]{2,1,0:T(8,128)}, u32[]{:S(2)}) %copy-start) | copy-done | bytes 1048600
  2.5 0.0 copy-start.1
  2.5 1.0 %copy-done.1 = f32[32,32,128]{2,1,0:T(8,128)S(1)} copy-done((f32[32,32,128]{2,1,0:T(8,128)S(1)}, f32[32,32,128]{2,1,0:T(8,128)}, u32[]{:S(2)}) %copy-start.1) | copy-done | bytes 524312
  3.6 0.0 copy-start.2
  3.6 1.0 %copy-done.2 = f32[32,32,128]{2,1,0:T(8,128)S(1)} copy-done((f32[32,32,128]{2,1,0:T(8,128)S(1)}, f32[32,32,128]{2,1,0:T(8,128)}, u32[]{:S(2)}) %copy-start.2) | copy-done | bytes 524312
  4.6 0.0 copy-start.3
  4.6 0.7 %copy-done.3 = s32[32,128]{1,0:T(8,128)S(1)} copy-done((s32[32,128]{1,0:T(8,128)S(1)}, s32[32,128]{1,0:T(8,128)}, u32[]{:S(2)}) %copy-start.3) | copy-done | bytes 16408
  5.3 32.5 %shard_map.84 = (f32[1024,128]{1,0:T(8,128)S(1)}, f32[1024,128]{1,0:T(8,128)S(1)}, f32[2048,128]{1,0:T(8,128)S(1)}, f32[32,32]{1,0:T(8,128)S(1)}) custom-call(f32[1024,128]{1,0:T(8,128)S(1)} %bitcast.8, f32[1024,128]{1,0:T(8,128)S(1)} %bitcast.9, f32[2048,128]{1,0:T(8,128)S(1)} %bitcast.7, s32[32,128]{1,0:T(8,128)S(1)} %copy-done.3, s32[1,128]{1,0:T(1,128)S(1)} %bitcast.10), custom_call_target="tpu_custom_call" | custom-call | tf_op jit(solution)/shard_map/pallas_call | solution.py:549
  37.9 1.4 %shard_map.85 = (f32[1024,128]{1,0:T(8,128)}, f32[1024,128]{1,0:T(8,128)}, f32[2048,128]{1,0:T(8,128)}, f32[32,32]{1,0:T(8,128)}) custom-call(f32[1024,128]{1,0:T(8,128)S(1)} %get-tuple-element.12.refs_0_, f32[1024,128]{1,0:T(8,128)S(1)} %get-tuple-element.13.refs_1_, f32[2048,128]{1,0:T(8,128)S(1)} %get-tuple-element.14.refs_2_, ...), custom_call_target="tpu_custom_call" | custom-call | tf_op jit(solution)/shard_map/pallas_call | solution.py:594
Async XLA Ops:
  0.6 0.7 %copy-start.4 = (s32[128]{0:T(128)S(1)}, s32[128]{0:T(128)}, u32[]{:S(2)}) copy-start(s32[128]{0:T(128)} %param.9) | copy-start | bytes 1540
  1.3 1.2 %copy-start = (f32[32,64,128]{2,1,0:T(8,128)S(1)}, f32[32,64,128]{2,1,0:T(8,128)}, u32[]{:S(2)}) copy-start(f32[32,64,128]{2,1,0:T(8,128)} %param.7) | copy-start | bytes 3145732
  2.5 1.0 %copy-start.1 = (f32[32,32,128]{2,1,0:T(8,128)S(1)}, f32[32,32,128]{2,1,0:T(8,128)}, u32[]{:S(2)}) copy-start(f32[32,32,128]{2,1,0:T(8,128)} %param.5) | copy-start | bytes 1572868
  3.6 1.0 %copy-start.2 = (f32[32,32,128]{2,1,0:T(8,128)S(1)}, f32[32,32,128]{2,1,0:T(8,128)}, u32[]{:S(2)}) copy-start(f32[32,32,128]{2,1,0:T(8,128)} %param.6) | copy-start | bytes 1572868
  4.6 0.7 %copy-start.3 = (s32[32,128]{1,0:T(8,128)S(1)}, s32[32,128]{1,0:T(8,128)}, u32[]{:S(2)}) copy-start(s32[32,128]{1,0:T(8,128)} %mask_ref.1) | copy-start | bytes 49156

commit v2 on v1

--- a/solution.py
+++ b/solution.py
@@ -1,4 +1,3 @@
-import functools
 import math
 
 import jax
@@ -20,7 +19,7 @@
 LAYERS = 64
 EXT = ROWS + 2 * SWEEPS
 HALF = ROWS // 2
-STRIP = HALF + 2 * SWEEPS
+STRIP = HALF + SWEEPS
 PACK = 10
 GROUPS = 3
 SOURCE_ROWS = 48
@@ -32,7 +31,8 @@
 C_UP, C_DOWN = 10, 11
 E_UP, E_DOWN = 12, 13
 S_UP, S_DOWN = 14, 15
-GATHER = 16
+CORNER = 16
+GATHER = 20
 
 
 def weight(sweep):
@@ -89,20 +89,26 @@
             carry = body(first + n * unroll + u, carry)
         return carry
 
-    carry = lax.fori_loop(0, count, several, carry)
+    carry = several(0, carry) if count == 1 else lax.fori_loop(0, count, several, carry)
     for row in range(first + count * unroll, last):
         carry = body(row, carry)
     return carry
 
 
-def copper_sweep(out, src, rhs, first, last, sweep):
+def after(src, row, cur, last, mirrored):
+    if mirrored and row == last - 1:
+        return roll(cur, 64)
+    return src[row + 1]
+
+
+def copper_sweep(out, src, rhs, first, last, sweep, mirrored=False):
     omega = weight(sweep)
     keep, gain = 1.0 - omega, omega / 7.0
     sub = sub_of((1, 8, LANES))
 
     def body(row, carry):
         prev, cur = carry
-        nxt = src[row + 1]
+        nxt = after(src, row, cur, last, mirrored)
         side = roll(cur, 1) + roll(cur, LANES - 1)
         up = jnp.concatenate(
             (cur[1:], jnp.where(sub == 7, 0.0, roll(cur[:1], 7, 1))), axis=0
@@ -114,11 +120,42 @@
         out[row] = keep * cur + gain * (rhs[row] + near)
         return cur, nxt
 
-    rows_loop(first, last, (last - first) // 2, body, (src[first - 1], src[first]))
+    unroll = last - first if last - first <= 16 else (last - first) // 2
+    rows_loop(first, last, unroll, body, (src[first - 1], src[first]))
+
+
+def source_row(source, row):
+    wide = jnp.broadcast_to(source[pl.ds(row, 1), :], (8, LANES))
+    return jnp.where(sub_of((8, LANES)) == 0, wide, 0.0)
+
+
+def response_sweep(out, src, source, first, last, sweep, mirrored=False):
+    omega = weight(sweep)
+    keep, gain = 1.0 - omega, omega / 7.0
+    sub = sub_of((8, LANES))
+
+    def begin(row, carry):
+        out[row] = gain * source_row(source, row)
+        return carry
+
+    def body(row, carry):
+        prev, cur = carry
+        nxt = after(src, row, cur, last, mirrored)
+        side = roll(cur, 1) + roll(cur, LANES - 1)
+        up = jnp.where(sub == 7, 0.0, roll(cur, 7, 0))
+        down = jnp.where(sub == 0, cur, roll(cur, 1, 0))
+        near = (prev + nxt) + (up + down) + side
+        out[row] = keep * cur + gain * (source_row(source, row) + near)
+        return cur, nxt
+
+    if sweep == 0:
+        rows_loop(first, last, last - first, begin, 0)
+    else:
+        rows_loop(first, last, last - first, body, (src[first - 1], src[first]))
 
 
 def edge_index(row):
-    n = lax.rem(row + STRIP - SWEEPS, STRIP)
+    n = jnp.where(row < SWEEPS, 2 * PACK + row, row - SWEEPS)
     group = n // PACK
     return group, SWEEPS * (n - group * PACK)
 
@@ -127,12 +164,12 @@
     v_in,
     t_in,
     c_in,
-    mask_ref,
-    shift_ref,
+    mask_in,
+    shift_in,
     v_out,
     t_out,
     c_out,
-    wall_ref,
+    wall_out,
     vb,
     tb,
     xn,
@@ -152,11 +189,24 @@
     surface,
     flux,
     source,
-    fix,
     strip_source,
     wall_send,
     wall_all,
     below,
+    mask_ref,
+    shift_ref,
+    corner_send,
+    corner_recv,
+    ov,
+    ot,
+    oc,
+    wall,
+    g0,
+    g1,
+    h0,
+    h1,
+    turned,
+    surface_new,
     send_sem,
     recv_sem,
     local_sem,
@@ -187,15 +237,20 @@
         pl.semaphore_signal(barrier, inc=1, device_id={"stream": lax.rem(i + m, streams)}, device_id_type=mesh_id)
     for other in (up_j, down_j):
         pl.semaphore_signal(barrier, inc=1, device_id={"span": other}, device_id_type=mesh_id)
+    for a in (up_i, down_i):
+        for b in (up_j, down_j):
+            pl.semaphore_signal(barrier, inc=1, device_id={"stream": a, "span": b}, device_id_type=mesh_id)
     for m in range(1, depths):
         pl.semaphore_signal(barrier, inc=1, device_id={"depth": lax.rem(k + m, depths)}, device_id_type=mesh_id)
 
     load_t = local(t_in, tb.at[pl.ds(CELLS, ROWS * CELLS)], 0)
     load_v = local(v_in, vb.at[pl.ds(CELLS, ROWS * CELLS)], 1)
     load_c = local(c_in, xn.at[pl.ds(SWEEPS * LAYERS, ROWS * LAYERS)], 2)
-    load_t.start()
-    load_c.start()
-    load_v.start()
+    load_mask = local(mask_in, mask_ref, 3)
+    load_shift = local(shift_in, shift_ref, 4)
+    loads = (load_t, load_c, load_v, load_mask, load_shift)
+    for c in loads:
+        c.start()
 
     lane32 = lane_of((CELLS, LANES))
     load_t.wait()
@@ -206,6 +261,8 @@
     load_v.wait()
     n_send[0] = vb[pl.ds(CELLS + CELLS - 1, ROWS, stride=CELLS), :]
     n_send[2] = vb[pl.ds(CELLS, ROWS, stride=CELLS), :]
+    load_mask.wait()
+    load_shift.wait()
 
     def pack_fluid(row, packed):
         at = pl.ds(pl.multiple_of(CELLS + row * CELLS, CELLS), CELLS)
@@ -217,7 +274,7 @@
 
     w_send[...] = rows_loop(0, ROWS, 8, pack_fluid, jnp.zeros((CELLS, LANES), jnp.float32))
 
-    pl.semaphore_wait(barrier, streams - 1 + 2 + depths - 1)
+    pl.semaphore_wait(barrier, streams - 1 + 2 + 4 + depths - 1)
 
     surfaces = [
         remote(surface.at[i], surface.at[i], GATHER + m, stream=lax.rem(i + m, streams))
@@ -259,8 +316,14 @@
         remote(xn.at[pl.ds(wide, wide)], xn.at[pl.ds(wide + ROWS * LAYERS, wide)], C_DOWN, stream=down_i),
     ]
     e_halos = [
-        remote(e_send.at[0], e_recv.at[0], E_UP, span=up_j),
-        remote(e_send.at[1], e_recv.at[1], E_DOWN, span=down_j),
+        remote(e_send.at[0], e_recv.at[0, pl.ds(0, 2)], E_UP, span=up_j),
+        remote(e_send.at[1], e_recv.at[1, pl.ds(0, 2)], E_DOWN, span=down_j),
+    ]
+    corners = [
+        remote(corner_send.at[0, 0], corner_recv.at[0], CORNER, stream=up_i, span=up_j),
+        remote(corner_send.at[0, 1], corner_recv.at[1], CORNER + 1, stream=down_i, span=up_j),
+        remote(corner_send.at[1, 0], corner_recv.at[2], CORNER + 2, stream=up_i, span=down_j),
+        remote(corner_send.at[1, 1], corner_recv.at[3], CORNER + 3, stream=down_i, span=down_j),
     ]
     s_halos = [
         remote(source.at[0], source.at[1], S_UP, span=up_j),
@@ -275,7 +338,15 @@
         for c in surfaces + planes:
             c.start()
 
-    for c in t_halos + v_halos + w_halos + n_halos + c_halos:
+    for c in t_halos:
+        c.start()
+
+    @pl.when(jnp.logical_not(is_bottom))
+    def _():
+        for c in c_halos:
+            c.start()
+
+    for c in v_halos + w_halos + n_halos:
         c.start()
 
     def arrange(row, carry):
@@ -290,10 +361,14 @@
     part = (lane8 & 63) // 16
     outer = jnp.logical_or(lane8 < 32, lane8 >= 96)
 
-    def edges(row, place, carry):
+    def ends_of(row, other):
+        return jnp.where(outer, rm[row], roll(rm[other], 64))
+
+    def keep_own(row, ends):
+        rs[row] = jnp.where(part == 1, roll(ends, 32), ends)
+
+    def pack(ends, place, carry):
         high, low = carry
-        ends = jnp.where(outer, rm[row], roll(rm[row + HALF], 64))
-        rs[row] = jnp.where(part == 1, roll(ends, 32), ends)
         chosen = jnp.logical_and((lane8 & 63) >= place, (lane8 & 63) < place + SWEEPS)
         return (
             jnp.where(chosen, roll(ends, place + SWEEPS), high),
@@ -302,12 +377,44 @@
 
     zero8 = jnp.zeros((8, 8, LANES), jnp.float32)
 
-    def edge_run(first, last, start, carry):
-        return rows_loop(first, last, 2, lambda row, c: edges(row, SWEEPS * (row - start), c), carry)
-
-    e_send[0, 0], e_send[1, 0] = edge_run(SWEEPS, SWEEPS + PACK, SWEEPS, (zero8, zero8))
-    middle = SWEEPS + PACK
-    e_send[0, 1], e_send[1, 1] = edge_run(middle, HALF + SWEEPS, middle, (zero8, zero8))
+    def pack_corner(n, carry):
+        return pack(ends_of(ROWS + n, 2 * SWEEPS - 1 - n), SWEEPS * n, carry)
+
+    halves = lane_of((4, 8, LANES)) < 64
+    for side, both in enumerate(rows_loop(0, SWEEPS, 3, pack_corner, (zero8, zero8))):
+        folded = both.reshape(4, 2, 8, LANES)
+        even, odd = folded[:, 0], folded[:, 1]
+        corner_send[side, 0] = jnp.where(halves, even, roll(odd, 64))
+        corner_send[side, 1] = jnp.where(halves, roll(even, 64), odd)
+    for group, count in enumerate((PACK, STRIP - SWEEPS - PACK)):
+
+        def pack_own(n, carry):
+            row = SWEEPS + group * PACK + n
+            ends = ends_of(row, EXT - 1 - row)
+            keep_own(row, ends)
+            return pack(ends, SWEEPS * n, carry)
+
+        e_send[0, group], e_send[1, group] = rows_loop(0, count, 2, pack_own, (zero8, zero8))
+
+    @pl.when(jnp.logical_not(is_bottom))
+    def _():
+        for c in e_halos + corners:
+            c.start()
+
+
+    def sweep_main(sweep, first, last):
+        a, b = (x0, x1) if sweep % 2 == 0 else (x1, x0)
+        copper_sweep(a, rm if sweep == 0 else b, rm, first, last, sweep)
+
+    def sweep_strip(sweep, first, last, mirrored=False):
+        a, b = (s0, s1) if sweep % 2 == 0 else (s1, s0)
+        copper_sweep(a, rs if sweep == 0 else b, rs, first, last, sweep, mirrored)
+
+    def sweep_inner(sweep):
+        sweep_main(sweep, SWEEPS + 1 + sweep, ROWS + SWEEPS - 1 - sweep)
+
+    for sweep in range(2):
+        sweep_inner(sweep)
 
     for c in t_halos:
         c.wait_recv()
@@ -338,18 +445,20 @@
         flux[i] = mask.astype(jnp.float32) * TRANSFER * (new - face_temp)
         for c in fluxes:
             c.start()
+        for c in c_halos + e_halos + corners:
+            c.start()
         below[0] = -v0
         below[1] = under
 
+    for sweep in range(2, SWEEPS):
+        sweep_inner(sweep)
+
+    n_halos[0].wait_recv()
+
     @pl.when(jnp.logical_not(is_bottom))
     def _():
-        n_halos[0].wait_recv()
         below[0] = n_recv[0]
         below[1] = n_recv[1]
-
-    @pl.when(is_bottom)
-    def _():
-        n_halos[0].wait_recv()
 
     for c in v_halos + w_halos + n_halos[1:]:
         c.wait_recv()
@@ -361,7 +470,7 @@
         base = pl.multiple_of(row * CELLS, CELLS)
         here = pl.ds(base + CELLS, CELLS)
         velocity = vb[here, :]
-        for field, (ref, out, coef) in enumerate(((vb, v_out, VISCOSITY), (tb, t_out, DIFFUSIVITY))):
+        for field, (ref, out, coef) in enumerate(((vb, ov, VISCOSITY), (tb, ot, DIFFUSIVITY))):
             x = velocity if field == 0 else ref[here, :]
             behind = ref[pl.ds(base, CELLS), :]
             ahead = ref[pl.ds(base + 2 * CELLS, CELLS), :]
@@ -380,17 +489,10 @@
 
     rows_loop(0, ROWS, 8, fluid, 0)
 
-    for c in c_halos:
-        c.wait_recv()
-    rows_loop(0, SWEEPS, 6, arrange, 0)
-    rows_loop(SWEEPS + ROWS, EXT, 6, arrange, 0)
-    carry = edge_run(HALF + SWEEPS, middle + PACK, middle, (e_send[0, 1], e_send[1, 1]))
-    e_send[0, 1], e_send[1, 1] = carry
-    carry = edge_run(middle + PACK, STRIP, middle + PACK, (zero8, zero8))
-    carry = edge_run(0, SWEEPS, middle + PACK - STRIP, carry)
-    e_send[0, 2], e_send[1, 2] = carry
-    for c in e_halos:
-        c.start()
+    store_v = local(ov, v_out, 5)
+    store_t = local(ot, t_out, 6)
+    store_v.start()
+    store_t.start()
 
     @pl.when(is_bottom)
     def _():
@@ -398,45 +500,8 @@
             c.wait_recv()
         amount = i * ROWS - SWEEPS - shift_ref[...]
         source[0] = route(flux[...].reshape(streams * ROWS, LANES), amount, SOURCE_ROWS)
-        for c in copies:
+        for c in copies + s_halos:
             c.start()
-
-    def sweep_main(sweep):
-        a, b = (x0, x1) if sweep % 2 == 0 else (x1, x0)
-        copper_sweep(a, rm if sweep == 0 else b, rm, 1 + sweep, EXT - 1 - sweep, sweep)
-
-    sweep_main(0)
-    sweep_main(1)
-
-    for m in range(1, depths):
-
-        @pl.when(k == m)
-        def _():
-            copies[m - 1].wait_recv()
-
-    for c in s_halos:
-        c.start()
-
-    heat = source[0]
-    gains = [weight(n) / 7.0 for n in range(2)]
-    once = gains[0] * heat
-    near = roll(once, 1, 0) + roll(once, SOURCE_ROWS - 1, 0) + roll(once, 1) + roll(once, LANES - 1) + once
-    fix[0] = (1.0 - weight(1)) * once + gains[1] * (heat + near)
-    fix[1] = gains[1] * once
-    top = sub_of((8, LANES)) == 0
-
-    def top_row(ref, row):
-        return jnp.where(top, jnp.broadcast_to(ref[pl.ds(row, 1), :], (8, LANES)), 0.0)
-
-    def mend(row, carry):
-        rm[row, 0] += top_row(source.at[0], row)
-        x1[row, 0] += top_row(fix.at[0], row)
-        x1[row, 1] += top_row(fix.at[1], row)
-        return carry
-
-    rows_loop(2, EXT - 2, 8, mend, 0)
-    for sweep in range(2, SWEEPS):
-        sweep_main(sweep)
 
     for c in e_halos:
         c.wait_recv()
@@ -448,36 +513,45 @@
         rs[row] = jnp.where(part == 2, east, jnp.where(part == 3, west, rs[row]))
         return carry
 
-    rows_loop(0, STRIP, 4, build, 0)
-    copper_sweep(s0, rs, rs, 1, STRIP - 1, 0)
-    for c in s_halos:
+    rows_loop(SWEEPS, STRIP, 4, build, 0)
+    for sweep in range(SWEEPS):
+        sweep_strip(sweep, SWEEPS + 1 + sweep, STRIP, True)
+
+    for c in c_halos:
         c.wait_recv()
-    lane = lane_of((32, LANES))
-    low0, low1 = source[0, pl.ds(0, 32), :], source[0, pl.ds(HALF, 32), :]
-    strip_source[...] = regions(
-        lane,
-        (
-            low0,
-            roll(low0, 32),
-            roll(source[2, pl.ds(0, 32), :], 32),
-            roll(source[1, pl.ds(HALF, 32), :], 64),
-            roll(low1, 64),
-            roll(low1, 96),
-            roll(source[2, pl.ds(HALF, 32), :], 96),
-            source[1, pl.ds(0, 32), :],
-        ),
-    )
-
-    def mend_strip(row, carry):
-        extra = top_row(strip_source, row)
-        rs[row, 0] += extra
-        s0[row, 0] += gains[0] * extra
-        return carry
-
-    rows_loop(1, STRIP - 1, 13, mend_strip, 0)
-    for sweep in range(1, SWEEPS):
-        a, b = (s0, s1) if sweep % 2 == 0 else (s1, s0)
-        copper_sweep(a, b, rs, 1 + sweep, STRIP - 1 - sweep, sweep)
+    rows_loop(0, SWEEPS, 6, arrange, 0)
+    rows_loop(SWEEPS + ROWS, EXT, 6, arrange, 0)
+
+    for c in corners:
+        c.wait_recv()
+    for side in range(2):
+        ups, downs = corner_recv[2 * side], corner_recv[2 * side + 1]
+        even = jnp.where(halves, ups, roll(downs, 64))
+        odd = jnp.where(halves, roll(ups, 64), downs)
+        e_recv[side, 2] = jnp.stack((even, odd), axis=1).reshape(8, 8, LANES)
+
+    def begin_strip(row, carry):
+        keep_own(row, ends_of(row, EXT - 1 - row))
+        return build(row, carry)
+
+    rows_loop(0, SWEEPS, 6, begin_strip, 0)
+    for sweep in range(SWEEPS):
+        sweep_main(sweep, 1 + sweep, SWEEPS + 1 + sweep)
+        sweep_main(sweep, ROWS + SWEEPS - 1 - sweep, EXT - 1 - sweep)
+        sweep_strip(sweep, 1 + sweep, SWEEPS + 1 + sweep)
+        if sweep == 3:
+            for m in range(1, depths):
+
+                @pl.when(k == m)
+                def _():
+                    copies[m - 1].wait_recv()
+                    for c in s_halos:
+                        c.start()
+
+
+    for sweep in range(SWEEPS):
+        a, b = (g0, g1) if sweep % 2 == 0 else (g1, g0)
+        response_sweep(a, b, source.at[0], 1 + sweep, EXT - 1 - sweep, sweep)
 
     def merged(lanes, main0, main1, strip):
         high = roll(strip, 96)
@@ -489,19 +563,42 @@
 
     lane1 = lane_of((8, LANES))
 
-    def assemble(n, carry):
-        halves = merged(lane8, x1[n + SWEEPS], x1[n + SWEEPS + HALF], s1[n + SWEEPS])
-        for half, done in enumerate(halves):
-            base = (n + half * HALF) * LAYERS
-            for r in range(8):
-                c_out[pl.ds(base + r, 8, stride=8), :] = done[r]
+    for c in s_halos:
+        c.wait_recv()
+
+    def turn(row, carry):
+        for side in range(3):
+            turned[side, pl.ds(row, 1), :] = source[side, pl.ds(EXT - 1 - row, 1), :]
         return carry
 
-    rows_loop(0, HALF, 4, assemble, 0)
+    rows_loop(0, STRIP + 2, 6, turn, 0)
+    lane = lane_of((STRIP + 2, LANES))
+    straight = pl.ds(0, STRIP + 2)
+    strip_source[...] = regions(
+        lane,
+        (
+            source[0, straight, :],
+            roll(source[0, straight, :], 32),
+            roll(source[2, straight, :], 32),
+            roll(turned[1], 64),
+            roll(turned[0], 64),
+            roll(turned[0], 96),
+            roll(turned[2], 96),
+            source[1, straight, :],
+        ),
+    )
+    for sweep in range(SWEEPS):
+        a, b = (h0, h1) if sweep % 2 == 0 else (h1, h0)
+        response_sweep(a, b, strip_source, 1 + sweep, STRIP, sweep, True)
 
     columns = LANES // depths
     tiles = ROWS // 8
-    new_surface = c_out[pl.ds(0, ROWS, stride=LAYERS), :]
+    for n in range(HALF):
+        low, high, edge = n + SWEEPS, EXT - 1 - SWEEPS - n, n + SWEEPS
+        both = merged(lane1, x1[low, 0] + g1[low], x1[high, 0] + g1[high], s1[edge, 0] + h1[edge])
+        surface_new[pl.ds(n, 1), :] = both[0][:1]
+        surface_new[pl.ds(ROWS - 1 - n, 1), :] = both[1][:1]
+    new_surface = surface_new[...]
     packed = jnp.zeros((8, LANES), jnp.float32)
     width = LANES // tiles
     for t in range(tiles):
@@ -512,12 +609,33 @@
         c.start()
     wall_all[i] = packed
     shift = roll(jnp.broadcast_to(shift_ref[...], (8, LANES)), lax.rem(LANES - columns * k, LANES))[:1]
+    def assemble(n, carry):
+        low, high = n, ROWS - 1 - n
+        both = merged(lane8, x1[low + SWEEPS], x1[high + SWEEPS], s1[n + SWEEPS])
+        for row, done in zip((low, high), both):
+            for r in range(8):
+                oc[pl.ds(row * LAYERS + r, 8, stride=8), :] = done[r]
+        return carry
+
+    rows_loop(0, HALF, 4, assemble, 0)
+    def add(n, carry):
+        low, high = n, ROWS - 1 - n
+        both = merged(lane1, g1[low + SWEEPS], g1[high + SWEEPS], h1[n + SWEEPS])
+        for row, more in zip((low, high), both):
+            oc[pl.ds(pl.multiple_of(row * LAYERS, LAYERS), 8), :] += more
+        return carry
+
+    rows_loop(0, HALF, 8, add, 0)
+    store_c = local(oc, c_out, 7)
+    store_c.start()
     for c in walls:
         c.wait_recv()
     rows = [roll(wall_all[b], LANES - width * t) for b in range(streams) for t in range(tiles)]
-    wall_ref[...] = route(jnp.concatenate(rows, axis=0), shift + i * ROWS, ROWS)[:, : wall_ref.shape[1]]
-
-    for c in t_halos + v_halos + w_halos + n_halos + c_halos + e_halos + s_halos + walls:
+    wall[...] = route(jnp.concatenate(rows, axis=0), shift + i * ROWS, ROWS)[:, :columns]
+    store_wall = local(wall, wall_out, 8)
+    store_wall.start()
+
+    for c in t_halos + v_halos + w_halos + n_halos + c_halos + e_halos + corners + s_halos + walls:
         c.wait_send()
 
     @pl.when(is_bottom)
@@ -525,26 +643,40 @@
         for c in surfaces + planes + fluxes + copies:
             c.wait_send()
 
+    for c in (store_v, store_t, store_c, store_wall):
+        c.wait()
+
 
 def write_out(*refs):
-    *sources, semaphores = refs
-    count = len(sources) // 2
-    copies = [
-        pltpu.make_async_copy(sources[n], sources[count + n], semaphores.at[n]) for n in range(count)
-    ]
-    for c in copies:
-        c.start()
-    for c in copies:
-        c.wait()
+    sources, results, stages = refs[:4], refs[4:8], refs[8:12]
+    semaphores = refs[12]
+    steps = []
+    for source, result, stage in zip(sources, results, stages):
+        rows = source.shape[0]
+        parts = max(1, rows // 512)
+        for part in range(parts):
+            at = pl.ds(part * (rows // parts), rows // parts)
+            read, write = semaphores.at[2 * len(steps)], semaphores.at[2 * len(steps) + 1]
+            steps.append(
+                (
+                    pltpu.make_async_copy(source.at[at], stage.at[at], read),
+                    pltpu.make_async_copy(stage.at[at], result.at[at], write),
+                )
+            )
+    for read, _ in steps:
+        read.start()
+    for read, write in steps:
+        read.wait()
+        write.start()
+    for _, write in steps:
+        write.wait()
 
 
 def per_device(fluid_velocity, fluid_temp, solid_temp, channel_mask, owner_shift):
     f32 = jnp.float32
     streams, depths = lax.axis_size("stream"), lax.axis_size("depth")
     fluid_rows, copper_rows = ROWS * CELLS, ROWS * LAYERS
-    vmem = pl.BlockSpec(memory_space=pltpu.VMEM)
     anywhere = pl.BlockSpec(memory_space=pl.ANY)
-    hbm = pl.BlockSpec(memory_space=pltpu.HBM)
     messages = GATHER + 3 * streams + depths
     outs = pl.pallas_call(
         kernel,
@@ -554,8 +686,8 @@
             jax.ShapeDtypeStruct((copper_rows, LANES), f32),
             jax.ShapeDtypeStruct((ROWS, LANES // depths), f32),
         ),
-        in_specs=[hbm, hbm, hbm, vmem, vmem],
-        out_specs=(vmem, vmem, vmem, vmem),
+        in_specs=[anywhere] * 5,
+        out_specs=(anywhere,) * 4,
         scratch_shapes=[
             pltpu.VMEM(((ROWS + 2) * CELLS, LANES), f32),
             pltpu.VMEM(((ROWS + 2) * CELLS, LANES), f32),
@@ -567,22 +699,33 @@
             pltpu.VMEM((CELLS, LANES), f32),
             pltpu.VMEM((2, CELLS, LANES), f32),
             pltpu.VMEM((2, ROWS, LANES), f32),
-            pltpu.VMEM((2, GROUPS, 8, 8, LANES), f32),
+            pltpu.VMEM((2, GROUPS - 1, 8, 8, LANES), f32),
             pltpu.VMEM((2, GROUPS, 8, 8, LANES), f32),
             pltpu.VMEM((streams, ROWS, LANES), f32),
             pltpu.VMEM((streams, ROWS, LANES), f32),
             pltpu.VMEM((3, SOURCE_ROWS, LANES), f32),
-            pltpu.VMEM((2, SOURCE_ROWS, LANES), f32),
-            pltpu.VMEM((32, LANES), f32),
+            pltpu.VMEM((STRIP + 2, LANES), f32),
             pltpu.VMEM((8, LANES), f32),
             pltpu.VMEM((streams, 8, LANES), f32),
             pltpu.VMEM((2, ROWS, LANES), f32),
+            pltpu.VMEM((ROWS, LANES), jnp.int32),
+            pltpu.VMEM((1, LANES), jnp.int32),
+            pltpu.VMEM((2, 2, 4, 8, LANES), f32),
+            pltpu.VMEM((4, 4, 8, LANES), f32),
+            pltpu.VMEM((fluid_rows, LANES), f32),
+            pltpu.VMEM((fluid_rows, LANES), f32),
+            pltpu.VMEM((copper_rows, LANES), f32),
+            pltpu.VMEM((ROWS, LANES // depths), f32),
+            *[pltpu.VMEM((EXT, 8, LANES), f32)] * 2,
+            *[pltpu.VMEM((STRIP, 8, LANES), f32)] * 2,
+            pltpu.VMEM((3, STRIP + 2, LANES), f32),
+            pltpu.VMEM((ROWS, LANES), f32),
             pltpu.SemaphoreType.DMA((messages,)),
             pltpu.SemaphoreType.DMA((messages,)),
-            pltpu.SemaphoreType.DMA((3,)),
+            pltpu.SemaphoreType.DMA((9,)),
         ],
         compiler_params=pltpu.CompilerParams(
-            collective_id=0, has_side_effects=True, vmem_limit_bytes=24 * 1024 * 1024
+            collective_id=0, has_side_effects=True, vmem_limit_bytes=57 * 1024 * 1024
         ),
     )(
         fluid_velocity.reshape(fluid_rows, LANES),
@@ -596,8 +739,8 @@
         out_shape=tuple(jax.ShapeDtypeStruct(o.shape, o.dtype) for o in outs),
         in_specs=[anywhere] * 4,
         out_specs=(anywhere,) * 4,
-        scratch_shapes=[pltpu.SemaphoreType.DMA((4,))],
-        compiler_params=pltpu.CompilerParams(vmem_limit_bytes=1024 * 1024),
+        scratch_shapes=[pltpu.VMEM(o.shape, o.dtype) for o in outs] + [pltpu.SemaphoreType.DMA((20,))],
+        compiler_params=pltpu.CompilerParams(vmem_limit_bytes=57 * 1024 * 1024),
     )(*outs)
     return (
         outs[0].reshape(fluid_velocity.shape),

time: 39.5 us -> 35.7 us (0.904)
  the two profiles are of different devices: /device:TPU:4 before, /device:TPU:1 now
where the time goes in v2:
time: 35.7 us; the launch traced here: 35.6 us
  Pallas kernels  34.9 us (98%)
  between operations  0.64 us (2%)
    pallas_call x1, Pallas kernels, per_device(): pl.pallas_call(kernel, out_shape=(jax.ShapeDtypeStruct((fluid_rows, LANES...  32.5 us
    pallas_call x1, Pallas kernels, per_device(): pl.pallas_call(write_out, out_shape=tuple((jax.ShapeDtypeStruct(o.shape,...  2.43 us

profile of v2, /device:TPU:1, one launch (start us, length us, event | category | flops | bytes accessed | tf_op | source)
XLA Modules:
  0.0 35.6 jit_solution(6699214015163744756)
XLA Ops:
  0.6 32.5 %shard_map.84 = (f32[1024,128]{1,0:T(8,128)}, f32[1024,128]{1,0:T(8,128)}, f32[2048,128]{1,0:T(8,128)}, f32[32,32]{1,0:T(8,128)}) custom-call(f32[1024,128]{1,0:T(8,128)} %bitcast.8, f32[1024,128]{1,0:T(8,128)} %bitcast.9, f32[2048,128]{1,0:T(8,128)} %bitcast.7, s32[32,128]{1,0:T(8,128)} %mask_in.1, s32[1,128]{1,0:T(1,128)} %bitcast.10), custom_call_target="tpu_custom_call" | custom-call | tf_op jit(solution)/shard_map/pallas_call | solution.py:681
  33.1 2.4 %shard_map.85 = (f32[1024,128]{1,0:T(8,128)}, f32[1024,128]{1,0:T(8,128)}, f32[2048,128]{1,0:T(8,128)}, f32[32,32]{1,0:T(8,128)}) custom-call(f32[1024,128]{1,0:T(8,128)} %get-tuple-element.12.refs_0_, f32[1024,128]{1,0:T(8,128)} %get-tuple-element.13.refs_1_, f32[2048,128]{1,0:T(8,128)} %get-tuple-element.14.refs_2_, f32[32,32]{1,0:T(8,128)} %get-tuple-element.15.refs_3_), custom_call_target="tpu_custom_call" | custom-call | tf_op jit(solution)/shard_map/pallas_call | solution.py:737

commit v3 on v2

--- a/solution.py
+++ b/solution.py
@@ -124,34 +124,33 @@
     rows_loop(first, last, unroll, body, (src[first - 1], src[first]))
 
 
-def source_row(source, row):
-    wide = jnp.broadcast_to(source[pl.ds(row, 1), :], (8, LANES))
-    return jnp.where(sub_of((8, LANES)) == 0, wide, 0.0)
-
-
-def response_sweep(out, src, source, first, last, sweep, mirrored=False):
-    omega = weight(sweep)
-    keep, gain = 1.0 - omega, omega / 7.0
-    sub = sub_of((8, LANES))
-
-    def begin(row, carry):
-        out[row] = gain * source_row(source, row)
-        return carry
-
-    def body(row, carry):
-        prev, cur = carry
-        nxt = after(src, row, cur, last, mirrored)
-        side = roll(cur, 1) + roll(cur, LANES - 1)
-        up = jnp.where(sub == 7, 0.0, roll(cur, 7, 0))
-        down = jnp.where(sub == 0, cur, roll(cur, 1, 0))
-        near = (prev + nxt) + (up + down) + side
-        out[row] = keep * cur + gain * (source_row(source, row) + near)
-        return cur, nxt
-
-    if sweep == 0:
-        rows_loop(first, last, last - first, begin, 0)
-    else:
-        rows_loop(first, last, last - first, body, (src[first - 1], src[first]))
+def response(source):
+    layers = [weight(0) / 7.0 * source]
+    rows = source.shape[0]
+    for sweep in range(1, SWEEPS):
+        omega = weight(sweep)
+        keep, gain = 1.0 - omega, omega / 7.0
+        new = []
+        for n in range(sweep + 1):
+            if n == sweep:
+                new.append(gain * layers[n - 1])
+                continue
+            cur = layers[n]
+            near = (roll(cur, 1, 0) + roll(cur, rows - 1, 0)) + (roll(cur, 1) + roll(cur, LANES - 1))
+            near += layers[n - 1] if n > 0 else cur + source
+            if n + 1 < sweep:
+                near += layers[n + 1]
+            new.append(keep * cur + gain * near)
+        layers = new
+    return layers
+
+
+def with_edges(main, strip):
+    lane = lane_of(main.shape)
+    first, second = strip[:HALF], strip[HALF:]
+    low = jnp.concatenate((first, roll(second, 64)), axis=0)
+    high = jnp.concatenate((roll(first, 96), roll(second, 32)), axis=0)
+    return jnp.where(lane < SWEEPS, low, jnp.where(lane >= LANES - SWEEPS, high, main))
 
 
 def edge_index(row):
@@ -189,7 +188,6 @@
     surface,
     flux,
     source,
-    strip_source,
     wall_send,
     wall_all,
     below,
@@ -201,12 +199,12 @@
     ot,
     oc,
     wall,
-    g0,
-    g1,
-    h0,
-    h1,
+    main_part,
+    strip_part,
+    strip_turned,
     turned,
-    surface_new,
+    main_top,
+    strip_top,
     send_sem,
     recv_sem,
     local_sem,
@@ -396,10 +394,8 @@
 
         e_send[0, group], e_send[1, group] = rows_loop(0, count, 2, pack_own, (zero8, zero8))
 
-    @pl.when(jnp.logical_not(is_bottom))
-    def _():
-        for c in e_halos + corners:
-            c.start()
+    for c in e_halos + corners:
+        c.start()
 
 
     def sweep_main(sweep, first, last):
@@ -445,7 +441,7 @@
         flux[i] = mask.astype(jnp.float32) * TRANSFER * (new - face_temp)
         for c in fluxes:
             c.start()
-        for c in c_halos + e_halos + corners:
+        for c in c_halos:
             c.start()
         below[0] = -v0
         below[1] = under
@@ -549,17 +545,14 @@
                         c.start()
 
 
-    for sweep in range(SWEEPS):
-        a, b = (g0, g1) if sweep % 2 == 0 else (g1, g0)
-        response_sweep(a, b, source.at[0], 1 + sweep, EXT - 1 - sweep, sweep)
-
-    def merged(lanes, main0, main1, strip):
-        high = roll(strip, 96)
-        other = roll(jnp.where(lanes < 64, high, strip), 64)
-        return tuple(
-            jnp.where(lanes < SWEEPS, low, jnp.where(lanes >= LANES - SWEEPS, up, main))
-            for low, up, main in ((strip, high, main0), (other, other, main1))
-        )
+    for n in range(HALF):
+        up, down = pl.ds(n, 1), pl.ds(ROWS - 1 - n, 1)
+        main_top[up, :] = x1[n + SWEEPS, 0, pl.ds(0, 1), :]
+        main_top[down, :] = x1[EXT - 1 - SWEEPS - n, 0, pl.ds(0, 1), :]
+        strip_top[up, :] = s1[n + SWEEPS, 0, pl.ds(0, 1), :]
+        strip_top[down, :] = s1[n + SWEEPS, 0, pl.ds(0, 1), :]
+    for n, plane in enumerate(response(source[0])):
+        main_part[n] = plane
 
     lane1 = lane_of((8, LANES))
 
@@ -571,11 +564,10 @@
             turned[side, pl.ds(row, 1), :] = source[side, pl.ds(EXT - 1 - row, 1), :]
         return carry
 
-    rows_loop(0, STRIP + 2, 6, turn, 0)
-    lane = lane_of((STRIP + 2, LANES))
-    straight = pl.ds(0, STRIP + 2)
-    strip_source[...] = regions(
-        lane,
+    rows_loop(0, ROWS, 8, turn, 0)
+    straight = pl.ds(0, ROWS)
+    strip_source = regions(
+        lane32,
         (
             source[0, straight, :],
             roll(source[0, straight, :], 32),
@@ -587,18 +579,20 @@
             source[1, straight, :],
         ),
     )
-    for sweep in range(SWEEPS):
-        a, b = (h0, h1) if sweep % 2 == 0 else (h1, h0)
-        response_sweep(a, b, strip_source, 1 + sweep, STRIP, sweep, True)
+    for n, plane in enumerate(response(strip_source)):
+        strip_part[n] = plane
+
+    def turn_part(n):
+        strip_turned[n, pl.ds(0, HALF), :] = strip_part[n, pl.ds(SWEEPS, HALF), :]
+        for row in range(HALF):
+            strip_turned[n, pl.ds(ROWS - 1 - row, 1), :] = strip_part[n, pl.ds(SWEEPS + row, 1), :]
+
+    turn_part(0)
+    inner = pl.ds(SWEEPS, ROWS)
 
     columns = LANES // depths
     tiles = ROWS // 8
-    for n in range(HALF):
-        low, high, edge = n + SWEEPS, EXT - 1 - SWEEPS - n, n + SWEEPS
-        both = merged(lane1, x1[low, 0] + g1[low], x1[high, 0] + g1[high], s1[edge, 0] + h1[edge])
-        surface_new[pl.ds(n, 1), :] = both[0][:1]
-        surface_new[pl.ds(ROWS - 1 - n, 1), :] = both[1][:1]
-    new_surface = surface_new[...]
+    new_surface = with_edges(main_top[...] + main_part[0, inner, :], strip_top[...] + strip_turned[0])
     packed = jnp.zeros((8, LANES), jnp.float32)
     width = LANES // tiles
     for t in range(tiles):
@@ -611,21 +605,22 @@
     shift = roll(jnp.broadcast_to(shift_ref[...], (8, LANES)), lax.rem(LANES - columns * k, LANES))[:1]
     def assemble(n, carry):
         low, high = n, ROWS - 1 - n
-        both = merged(lane8, x1[low + SWEEPS], x1[high + SWEEPS], s1[n + SWEEPS])
-        for row, done in zip((low, high), both):
+        strip = s1[n + SWEEPS]
+        right = roll(strip, 96)
+        other = roll(jnp.where(lane8 < 64, right, strip), 64)
+        for row, left, end in ((low, strip, right), (high, other, other)):
+            main = x1[row + SWEEPS]
+            done = jnp.where(lane8 < SWEEPS, left, jnp.where(lane8 >= LANES - SWEEPS, end, main))
             for r in range(8):
                 oc[pl.ds(row * LAYERS + r, 8, stride=8), :] = done[r]
         return carry
 
     rows_loop(0, HALF, 4, assemble, 0)
-    def add(n, carry):
-        low, high = n, ROWS - 1 - n
-        both = merged(lane1, g1[low + SWEEPS], g1[high + SWEEPS], h1[n + SWEEPS])
-        for row, more in zip((low, high), both):
-            oc[pl.ds(pl.multiple_of(row * LAYERS, LAYERS), 8), :] += more
-        return carry
-
-    rows_loop(0, HALF, 8, add, 0)
+    for n in range(SWEEPS):
+        if n > 0:
+            turn_part(n)
+        layer = pl.ds(n, ROWS, stride=LAYERS)
+        oc[layer, :] += with_edges(main_part[n, inner, :], strip_turned[n])
     store_c = local(oc, c_out, 7)
     store_c.start()
     for c in walls:
@@ -704,7 +699,6 @@
             pltpu.VMEM((streams, ROWS, LANES), f32),
             pltpu.VMEM((streams, ROWS, LANES), f32),
             pltpu.VMEM((3, SOURCE_ROWS, LANES), f32),
-            pltpu.VMEM((STRIP + 2, LANES), f32),
             pltpu.VMEM((8, LANES), f32),
             pltpu.VMEM((streams, 8, LANES), f32),
             pltpu.VMEM((2, ROWS, LANES), f32),
@@ -716,9 +710,11 @@
             pltpu.VMEM((fluid_rows, LANES), f32),
             pltpu.VMEM((copper_rows, LANES), f32),
             pltpu.VMEM((ROWS, LANES // depths), f32),
-            *[pltpu.VMEM((EXT, 8, LANES), f32)] * 2,
-            *[pltpu.VMEM((STRIP, 8, LANES), f32)] * 2,
-            pltpu.VMEM((3, STRIP + 2, LANES), f32),
+            pltpu.VMEM((SWEEPS, SOURCE_ROWS, LANES), f32),
+            pltpu.VMEM((SWEEPS, ROWS, LANES), f32),
+            pltpu.VMEM((SWEEPS, ROWS, LANES), f32),
+            pltpu.VMEM((3, ROWS, LANES), f32),
+            pltpu.VMEM((ROWS, LANES), f32),
             pltpu.VMEM((ROWS, LANES), f32),
             pltpu.SemaphoreType.DMA((messages,)),
             pltpu.SemaphoreType.DMA((messages,)),

time: 35.7 us -> 32.9 us (0.922)
  the two profiles are of different devices: /device:TPU:1 before, /device:TPU:0 now
where the time goes in v3:
time: 32.9 us; the launch traced here: 32.7 us
  Pallas kernels  32 us (97%)
  between operations  0.64 us (2%)
    pallas_call x1, Pallas kernels, per_device(): pl.pallas_call(kernel, out_shape=(jax.ShapeDtypeStruct((fluid_rows, LANES...  29.6 us
    pallas_call x1, Pallas kernels, per_device(): pl.pallas_call(write_out, out_shape=tuple((jax.ShapeDtypeStruct(o.shape,...  2.43 us

profile of v3, /device:TPU:0, one launch (start us, length us, event | category | flops | bytes accessed | tf_op | source)
XLA Modules:
  0.0 32.7 jit_solution(9493666136572427646)
XLA Ops:
  0.6 29.6 %shard_map.84 = (f32[1024,128]{1,0:T(8,128)}, f32[1024,128]{1,0:T(8,128)}, f32[2048,128]{1,0:T(8,128)}, f32[32,32]{1,0:T(8,128)}) custom-call(f32[1024,128]{1,0:T(8,128)} %bitcast.8, f32[1024,128]{1,0:T(8,128)} %bitcast.9, f32[2048,128]{1,0:T(8,128)} %bitcast.7, s32[32,128]{1,0:T(8,128)} %mask_in.1, s32[1,128]{1,0:T(1,128)} %bitcast.10), custom_call_target="tpu_custom_call" | custom-call | tf_op jit(solution)/shard_map/pallas_call | solution.py:676
  30.2 2.4 %shard_map.85 = (f32[1024,128]{1,0:T(8,128)}, f32[1024,128]{1,0:T(8,128)}, f32[2048,128]{1,0:T(8,128)}, f32[32,32]{1,0:T(8,128)}) custom-call(f32[1024,128]{1,0:T(8,128)} %get-tuple-element.12.refs_0_, f32[1024,128]{1,0:T(8,128)} %get-tuple-element.13.refs_1_, f32[2048,128]{1,0:T(8,128)} %get-tuple-element.14.refs_2_, f32[32,32]{1,0:T(8,128)} %get-tuple-element.15.refs_3_), custom_call_target="tpu_custom_call" | custom-call | tf_op jit(solution)/shard_map/pallas_call | solution.py:733

commit v4 on v3

--- a/solution.py
+++ b/solution.py
@@ -252,15 +252,89 @@
 
     lane32 = lane_of((CELLS, LANES))
     load_t.wait()
-    n_send[1] = tb[pl.ds(CELLS + CELLS - 1, ROWS, stride=CELLS), :]
     n_send[3] = tb[pl.ds(CELLS, ROWS, stride=CELLS), :]
     load_c.wait()
     surface[i] = xn[pl.ds(SWEEPS * LAYERS, ROWS, stride=LAYERS), :]
+    pl.semaphore_wait(barrier, streams - 1 + 2 + 4 + depths - 1)
+
+    surfaces = [
+        remote(surface.at[i], surface.at[i], GATHER + m, stream=lax.rem(i + m, streams))
+        for m in range(1, streams)
+    ]
+    fluxes = [
+        remote(flux.at[i], flux.at[i], GATHER + streams + m, stream=lax.rem(i + m, streams))
+        for m in range(1, streams)
+    ]
+    walls = [
+        remote(wall_send, wall_all.at[i], GATHER + 2 * streams + m, stream=lax.rem(i + m, streams))
+        for m in range(1, streams)
+    ]
+    planes = [
+        remote(n_send.at[3], t0_recv.at[0], T0_UP, span=up_j),
+        remote(n_send.at[3], t0_recv.at[1], T0_DOWN, span=down_j),
+    ]
+    last, first = pl.ds(ROWS * CELLS, CELLS), pl.ds(CELLS, CELLS)
+    before, after = pl.ds(0, CELLS), pl.ds((ROWS + 1) * CELLS, CELLS)
+    t_halos = [
+        remote(tb.at[last], tb.at[before], T_UP, stream=up_i),
+        remote(tb.at[first], tb.at[after], T_DOWN, stream=down_i),
+    ]
+    v_halos = [
+        remote(vb.at[last], vb.at[before], V_UP, stream=up_i),
+        remote(vb.at[first], vb.at[after], V_DOWN, stream=down_i),
+    ]
+    n_halos = [
+        remote(n_send.at[pl.ds(0, 2)], n_recv.at[pl.ds(0, 2)], N_UP, depth=up_k),
+        remote(n_send.at[pl.ds(2, 2)], n_recv.at[pl.ds(2, 2)], N_DOWN, depth=down_k),
+    ]
+    w_halos = [
+        remote(w_send, w_recv.at[0], W_UP, span=up_j),
+        remote(w_send, w_recv.at[1], W_DOWN, span=down_j),
+    ]
+    wide = SWEEPS * LAYERS
+    c_halos = [
+        remote(xn.at[pl.ds(ROWS * LAYERS, wide)], xn.at[pl.ds(0, wide)], C_UP, stream=up_i),
+        remote(xn.at[pl.ds(wide, wide)], xn.at[pl.ds(wide + ROWS * LAYERS, wide)], C_DOWN, stream=down_i),
+    ]
+    e_halos = [
+        remote(e_send.at[0], e_recv.at[0, pl.ds(0, 2)], E_UP, span=up_j),
+        remote(e_send.at[1], e_recv.at[1, pl.ds(0, 2)], E_DOWN, span=down_j),
+    ]
+    corners = [
+        remote(corner_send.at[0, 0], corner_recv.at[0], CORNER, stream=up_i, span=up_j),
+        remote(corner_send.at[0, 1], corner_recv.at[1], CORNER + 1, stream=down_i, span=up_j),
+        remote(corner_send.at[1, 0], corner_recv.at[2], CORNER + 2, stream=up_i, span=down_j),
+        remote(corner_send.at[1, 1], corner_recv.at[3], CORNER + 3, stream=down_i, span=down_j),
+    ]
+    s_halos = [
+        remote(source.at[0], source.at[1], S_UP, span=up_j),
+        remote(source.at[0], source.at[2], S_DOWN, span=down_j),
+    ]
+    copies = [
+        remote(source.at[0], source.at[0], GATHER + 3 * streams + m, depth=m) for m in range(1, depths)
+    ]
+
+    @pl.when(is_bottom)
+    def _():
+        for c in surfaces + planes:
+            c.start()
+
+    for c in t_halos:
+        c.start()
+
+    @pl.when(jnp.logical_not(is_bottom))
+    def _():
+        for c in c_halos:
+            c.start()
+
+    n_send[1] = tb[pl.ds(CELLS + CELLS - 1, ROWS, stride=CELLS), :]
     load_v.wait()
     n_send[0] = vb[pl.ds(CELLS + CELLS - 1, ROWS, stride=CELLS), :]
     n_send[2] = vb[pl.ds(CELLS, ROWS, stride=CELLS), :]
     load_mask.wait()
     load_shift.wait()
+    for c in v_halos + n_halos:
+        c.start()
 
     def pack_fluid(row, packed):
         at = pl.ds(pl.multiple_of(CELLS + row * CELLS, CELLS), CELLS)
@@ -272,79 +346,7 @@
 
     w_send[...] = rows_loop(0, ROWS, 8, pack_fluid, jnp.zeros((CELLS, LANES), jnp.float32))
 
-    pl.semaphore_wait(barrier, streams - 1 + 2 + 4 + depths - 1)
-
-    surfaces = [
-        remote(surface.at[i], surface.at[i], GATHER + m, stream=lax.rem(i + m, streams))
-        for m in range(1, streams)
-    ]
-    fluxes = [
-        remote(flux.at[i], flux.at[i], GATHER + streams + m, stream=lax.rem(i + m, streams))
-        for m in range(1, streams)
-    ]
-    walls = [
-        remote(wall_send, wall_all.at[i], GATHER + 2 * streams + m, stream=lax.rem(i + m, streams))
-        for m in range(1, streams)
-    ]
-    planes = [
-        remote(n_send.at[3], t0_recv.at[0], T0_UP, span=up_j),
-        remote(n_send.at[3], t0_recv.at[1], T0_DOWN, span=down_j),
-    ]
-    last, first = pl.ds(ROWS * CELLS, CELLS), pl.ds(CELLS, CELLS)
-    before, after = pl.ds(0, CELLS), pl.ds((ROWS + 1) * CELLS, CELLS)
-    t_halos = [
-        remote(tb.at[last], tb.at[before], T_UP, stream=up_i),
-        remote(tb.at[first], tb.at[after], T_DOWN, stream=down_i),
-    ]
-    v_halos = [
-        remote(vb.at[last], vb.at[before], V_UP, stream=up_i),
-        remote(vb.at[first], vb.at[after], V_DOWN, stream=down_i),
-    ]
-    n_halos = [
-        remote(n_send.at[pl.ds(0, 2)], n_recv.at[pl.ds(0, 2)], N_UP, depth=up_k),
-        remote(n_send.at[pl.ds(2, 2)], n_recv.at[pl.ds(2, 2)], N_DOWN, depth=down_k),
-    ]
-    w_halos = [
-        remote(w_send, w_recv.at[0], W_UP, span=up_j),
-        remote(w_send, w_recv.at[1], W_DOWN, span=down_j),
-    ]
-    wide = SWEEPS * LAYERS
-    c_halos = [
-        remote(xn.at[pl.ds(ROWS * LAYERS, wide)], xn.at[pl.ds(0, wide)], C_UP, stream=up_i),
-        remote(xn.at[pl.ds(wide, wide)], xn.at[pl.ds(wide + ROWS * LAYERS, wide)], C_DOWN, stream=down_i),
-    ]
-    e_halos = [
-        remote(e_send.at[0], e_recv.at[0, pl.ds(0, 2)], E_UP, span=up_j),
-        remote(e_send.at[1], e_recv.at[1, pl.ds(0, 2)], E_DOWN, span=down_j),
-    ]
-    corners = [
-        remote(corner_send.at[0, 0], corner_recv.at[0], CORNER, stream=up_i, span=up_j),
-        remote(corner_send.at[0, 1], corner_recv.at[1], CORNER + 1, stream=down_i, span=up_j),
-        remote(corner_send.at[1, 0], corner_recv.at[2], CORNER + 2, stream=up_i, span=down_j),
-        remote(corner_send.at[1, 1], corner_recv.at[3], CORNER + 3, stream=down_i, span=down_j),
-    ]
-    s_halos = [
-        remote(source.at[0], source.at[1], S_UP, span=up_j),
-        remote(source.at[0], source.at[2], S_DOWN, span=down_j),
-    ]
-    copies = [
-        remote(source.at[0], source.at[0], GATHER + 3 * streams + m, depth=m) for m in range(1, depths)
-    ]
-
-    @pl.when(is_bottom)
-    def _():
-        for c in surfaces + planes:
-            c.start()
-
-    for c in t_halos:
-        c.start()
-
-    @pl.when(jnp.logical_not(is_bottom))
-    def _():
-        for c in c_halos:
-            c.start()
-
-    for c in v_halos + w_halos + n_halos:
+    for c in w_halos:
         c.start()
 
     def arrange(row, carry):
@@ -449,47 +451,19 @@
     for sweep in range(2, SWEEPS):
         sweep_inner(sweep)
 
-    n_halos[0].wait_recv()
-
-    @pl.when(jnp.logical_not(is_bottom))
-    def _():
-        below[0] = n_recv[0]
-        below[1] = n_recv[1]
-
-    for c in v_halos + w_halos + n_halos[1:]:
+    for c in e_halos:
         c.wait_recv()
 
-    sub32 = sub_of((CELLS, LANES))
-    w_all = jnp.where((lane32 & 1) == 0, roll(w_recv[0], 1), roll(w_recv[1], LANES - 1))
-
-    def fluid(row, carry):
-        base = pl.multiple_of(row * CELLS, CELLS)
-        here = pl.ds(base + CELLS, CELLS)
-        velocity = vb[here, :]
-        for field, (ref, out, coef) in enumerate(((vb, ov, VISCOSITY), (tb, ot, DIFFUSIVITY))):
-            x = velocity if field == 0 else ref[here, :]
-            behind = ref[pl.ds(base, CELLS), :]
-            ahead = ref[pl.ds(base + 2 * CELLS, CELLS), :]
-            ends = roll(w_all, lax.rem(LANES - 2 * row, LANES) if field == 0 else 64 - 2 * row)
-            west = jnp.where(lane32 == 0, ends, roll(x, 1))
-            east = jnp.where(lane32 == LANES - 1, ends, roll(x, LANES - 1))
-            under = jnp.broadcast_to(below[field, pl.ds(row, 1), :], (CELLS, LANES))
-            over = jnp.where(is_top, x[CELLS - 1 :], n_recv[2 + field, pl.ds(row, 1), :])
-            over = jnp.broadcast_to(over, (CELLS, LANES))
-            lower = jnp.where(sub32 == 0, under, roll(x, 1, 0))
-            upper = jnp.where(sub32 == CELLS - 1, over, roll(x, CELLS - 1, 0))
-            lap = (ahead + behind) + (west + east) + (lower + upper) - 6.0 * x
-            grad = (ahead - behind) * 0.5
-            out[pl.ds(base, CELLS), :] = x + coef * lap - ADVECTION * velocity * grad
+    def build(row, carry):
+        group, place = edge_index(row)
+        east = roll(e_recv[1, group], lax.rem(LANES + 32 - place, LANES))
+        west = roll(e_recv[0, group], 122 - place)
+        rs[row] = jnp.where(part == 2, east, jnp.where(part == 3, west, rs[row]))
         return carry
 
-    rows_loop(0, ROWS, 8, fluid, 0)
-
-    store_v = local(ov, v_out, 5)
-    store_t = local(ot, t_out, 6)
-    store_v.start()
-    store_t.start()
-
+    rows_loop(SWEEPS, STRIP, 4, build, 0)
+    for sweep in range(SWEEPS):
+        sweep_strip(sweep, SWEEPS + 1 + sweep, STRIP, True)
     @pl.when(is_bottom)
     def _():
         for c in fluxes:
@@ -499,19 +473,6 @@
         for c in copies + s_halos:
             c.start()
 
-    for c in e_halos:
-        c.wait_recv()
-
-    def build(row, carry):
-        group, place = edge_index(row)
-        east = roll(e_recv[1, group], lax.rem(LANES + 32 - place, LANES))
-        west = roll(e_recv[0, group], 122 - place)
-        rs[row] = jnp.where(part == 2, east, jnp.where(part == 3, west, rs[row]))
-        return carry
-
-    rows_loop(SWEEPS, STRIP, 4, build, 0)
-    for sweep in range(SWEEPS):
-        sweep_strip(sweep, SWEEPS + 1 + sweep, STRIP, True)
 
     for c in c_halos:
         c.wait_recv()
@@ -623,6 +584,48 @@
         oc[layer, :] += with_edges(main_part[n, inner, :], strip_turned[n])
     store_c = local(oc, c_out, 7)
     store_c.start()
+
+    n_halos[0].wait_recv()
+
+    @pl.when(jnp.logical_not(is_bottom))
+    def _():
+        below[0] = n_recv[0]
+        below[1] = n_recv[1]
+
+    for c in v_halos + w_halos + n_halos[1:]:
+        c.wait_recv()
+
+    sub32 = sub_of((CELLS, LANES))
+    w_all = jnp.where((lane32 & 1) == 0, roll(w_recv[0], 1), roll(w_recv[1], LANES - 1))
+
+    def fluid(row, carry):
+        base = pl.multiple_of(row * CELLS, CELLS)
+        here = pl.ds(base + CELLS, CELLS)
+        velocity = vb[here, :]
+        for field, (ref, out, coef) in enumerate(((vb, ov, VISCOSITY), (tb, ot, DIFFUSIVITY))):
+            x = velocity if field == 0 else ref[here, :]
+            behind = ref[pl.ds(base, CELLS), :]
+            ahead = ref[pl.ds(base + 2 * CELLS, CELLS), :]
+            ends = roll(w_all, lax.rem(LANES - 2 * row, LANES) if field == 0 else 64 - 2 * row)
+            west = jnp.where(lane32 == 0, ends, roll(x, 1))
+            east = jnp.where(lane32 == LANES - 1, ends, roll(x, LANES - 1))
+            under = jnp.broadcast_to(below[field, pl.ds(row, 1), :], (CELLS, LANES))
+            over = jnp.where(is_top, x[CELLS - 1 :], n_recv[2 + field, pl.ds(row, 1), :])
+            over = jnp.broadcast_to(over, (CELLS, LANES))
+            lower = jnp.where(sub32 == 0, under, roll(x, 1, 0))
+            upper = jnp.where(sub32 == CELLS - 1, over, roll(x, CELLS - 1, 0))
+            lap = (ahead + behind) + (west + east) + (lower + upper) - 6.0 * x
+            grad = (ahead - behind) * 0.5
+            out[pl.ds(base, CELLS), :] = x + coef * lap - ADVECTION * velocity * grad
+        return carry
+
+    rows_loop(0, ROWS, 8, fluid, 0)
+
+    store_v = local(ov, v_out, 5)
+    store_t = local(ot, t_out, 6)
+    store_v.start()
+    store_t.start()
+
     for c in walls:
         c.wait_recv()
     rows = [roll(wall_all[b], LANES - width * t) for b in range(streams) for t in range(tiles)]

time: 32.9 us -> 32.8 us (level)
  no operation moved by 1% of the time
where the time goes in v4:
time: 32.8 us; the launch traced here: 32.7 us
  Pallas kernels  32 us (98%)
  between operations  0.64 us (2%)
    pallas_call x1, Pallas kernels, per_device(): pl.pallas_call(kernel, out_shape=(jax.ShapeDtypeStruct((fluid_rows, LANES...  29.6 us
    pallas_call x1, Pallas kernels, per_device(): pl.pallas_call(write_out, out_shape=tuple((jax.ShapeDtypeStruct(o.shape,...  2.43 us

profile of v4, /device:TPU:0, one launch (start us, length us, event | category | flops | bytes accessed | tf_op | source)
XLA Modules:
  0.0 32.7 jit_solution(11540636200444979123)
XLA Ops:
  0.6 29.6 %shard_map.84 = (f32[1024,128]{1,0:T(8,128)}, f32[1024,128]{1,0:T(8,128)}, f32[2048,128]{1,0:T(8,128)}, f32[32,32]{1,0:T(8,128)}) custom-call(f32[1024,128]{1,0:T(8,128)} %bitcast.8, f32[1024,128]{1,0:T(8,128)} %bitcast.9, f32[2048,128]{1,0:T(8,128)} %bitcast.7, s32[32,128]{1,0:T(8,128)} %mask_in.1, s32[1,128]{1,0:T(1,128)} %bitcast.10), custom_call_target="tpu_custom_call" | custom-call | tf_op jit(solution)/shard_map/pallas_call | solution.py:679
  30.2 2.4 %shard_map.85 = (f32[1024,128]{1,0:T(8,128)}, f32[1024,128]{1,0:T(8,128)}, f32[2048,128]{1,0:T(8,128)}, f32[32,32]{1,0:T(8,128)}) custom-call(f32[1024,128]{1,0:T(8,128)} %get-tuple-element.12.refs_0_, f32[1024,128]{1,0:T(8,128)} %get-tuple-element.13.refs_1_, f32[2048,128]{1,0:T(8,128)} %get-tuple-element.14.refs_2_, f32[32,32]{1,0:T(8,128)} %get-tuple-element.15.refs_3_), custom_call_target="tpu_custom_call" | custom-call | tf_op jit(solution)/shard_map/pallas_call | solution.py:736
